TPU v7x, 512 devices: a whole 4x4x16 slice. The times are simulated.
512 devices in a mesh: grp: 64 (over z, x), sub: 4 (over y), rep: 2 (over core).
Axes of the slice: x: 4, y: 4, z: 16, core: 2. Of those that a mesh axis runs over, the one named last changes fastest.
Arguments:
- starting_concentration_per_run: float32 [64, 8, 256, 512], P('grp', None, 'sub', 'rep'), may hold values from -6 to 6
- diffusivity: float32 [256, 512], P('sub', 'rep'), may hold values from 0.02 to 0.12
- run_layer_stability_number: float32 [64, 8], P('grp'), may hold values from 0.05 to 0.4
- observed: float32 [256, 4, 128], P(('sub', 'grp'), 'rep'), may hold values from -6 to 6
- slot_error_variance: float32 [256, 4, 128], P(('sub', 'grp'), 'rep'), may hold values from 0.25 to 4
- sensor_target_site: int32 [256, 4, 128], P(('sub', 'grp'), 'rep'), may hold values from 0 to 1023
- patch_live_count: int32 [256, 4], P(('sub', 'grp'), 'rep'), may hold values from 1 to 128, as said below
Outputs:
- analysis: float32 [64, 8, 256, 512], P('grp', None, 'sub', 'rep')
Inputs may be any that keep to these rules, and one draw needn't show every extreme that they name: Slots below patch_live_count of a patch are live, the rest are unused; some patch has all 128 slots live. `sensor_target_site`: A slot observes the cell level * 128 + column of its own patch.
All inputs are finite; a program needn't handle non-finite values.
Results may differ from a plain program's by a relative error of at most 0.0003.
Values sent between devices are 32-bit elements; how exact they have to be, the bound alone decides.
No kernel may reach another device: no remote copies, remote signals or barrier semaphores. Data moves between devices by JAX's collectives and lax.ppermute only.
A program may use at most 64 MiB of HBM per device.

v0:
```python
import jax
import jax.numpy as jnp
from jax import lax
from jax.sharding import Mesh
from jax.sharding import PartitionSpec as P

PATCH = 128
STEPS = 4
NS_ITERS = 4
GRP = ("grp_0", "grp_1")
SUB_GRP = ("sub", "grp_0", "grp_1")


HIGHEST = lax.Precision.HIGHEST


def extended_2(x, sides, width):
    for axis, dim in sides:
        devices, length = (lax.axis_size(axis), x.shape[dim])
        up = [(i, (i + 1) % devices) for i in range(devices - 1)]
        down = [(j, i) for i, j in up]
        last = lax.slice_in_dim(x, length - width, length, axis=dim)
        initial = lax.slice_in_dim(x, 0, width, axis=dim)
        before = lax.ppermute(last, axis, up)
        after = lax.ppermute(initial, axis, down)
        x = jnp.concatenate([before, x, after], axis=dim)
    return x


def in_blocks(x, dim, devices):
    dims = x.shape
    parts = x.reshape(*dims[:dim], devices, dims[dim] // devices, *dims[dim + 1 :])
    return jnp.moveaxis(parts, dim, 0)


def laid_out(parts, dim):
    parts = jnp.moveaxis(parts, 0, dim)
    dims = parts.shape
    return parts.reshape(*dims[:dim], dims[dim] * dims[dim + 1], *dims[dim + 2 :])


def moved_by_axis(parts, axes, turns):
    dims = [lax.axis_size(a) for a in axes]
    parts = parts.reshape(*dims, *parts.shape[1:])
    for k in turns:
        parts = lax.all_to_all(parts, axes[k], split_axis=k, concat_axis=k, tiled=True)
    return parts.reshape(-1, *parts.shape[len(axes) :])


def one_axis_at_a_time(x, axes, turns, split_dim, concat_dim):
    parts = in_blocks(x, split_dim, lax.axis_size(axes))
    return laid_out(moved_by_axis(parts, axes, turns), concat_dim)


def advance(padded, diffusivity, member_wind):
    centre = padded[..., 1:-1, 1:-1]
    northern = padded[..., :-2, 1:-1]
    southern = padded[..., 2:, 1:-1]
    western = padded[..., 1:-1, :-2]
    easterly_side = padded[..., 1:-1, 2:]
    spread = northern + southern + (western + easterly_side) - 4.0 * centre
    return centre + diffusivity * spread - member_wind * (centre - western)


def analyse(background, sampled, observed, slot_error_variance, patch_live_count):
    members = background.shape[1]
    slots = observed.shape[-1]
    centre_mean = jnp.mean(background, axis=1, keepdims=True)
    perturbed = background - centre_mean
    sampled_mean = jnp.mean(sampled, axis=1, keepdims=True)
    sampled_pert = sampled - sampled_mean
    live_slot = jnp.arange(slots)[None, :] < patch_live_count[:, None]
    precision_obs = jnp.where(live_slot, 1.0 / slot_error_variance, 0.0 * slot_error_variance)
    innovation = observed - sampled_mean[:, 0, :]
    weighted = sampled_pert * precision_obs[:, None, :]
    identity = jnp.eye(members, dtype=background.dtype)
    system = (
        jnp.einsum("pms,pns->pmn", weighted, sampled_pert, precision=HIGHEST)
        + (members - 1.0) * identity
    )
    source_term = jnp.einsum("pms,ps->pm", weighted, innovation, precision=HIGHEST)
    factor = jnp.linalg.cholesky(system)
    halfway = lax.linalg.triangular_solve(
        factor, source_term[:, :, None], left_side=True, lower=True
    )
    mean_weight = lax.linalg.triangular_solve(
        factor, halfway, left_side=True, lower=True, transpose_a=True
    )[:, :, 0]
    norm_scale = jnp.sqrt(jnp.sum(system * system, axis=(1, 2)))
    iterate = system / norm_scale[:, None, None]
    inverse_root = jnp.broadcast_to(identity, system.shape)
    for sweep in range(NS_ITERS):
        update = 1.5 * identity - 0.5 * jnp.einsum(
            "pij,pjk->pik", inverse_root, iterate, precision=HIGHEST
        )
        iterate = jnp.einsum("pij,pjk->pik", iterate, update, precision=HIGHEST)
        inverse_root = jnp.einsum("pij,pjk->pik", update, inverse_root, precision=HIGHEST)
    spread_weight = inverse_root * jnp.sqrt((members - 1.0) / norm_scale)[:, None, None]
    combined = spread_weight + mean_weight[:, :, None]
    return centre_mean + jnp.einsum("pki,pkc->pic", combined, perturbed, precision=HIGHEST)


def on_device(
    starting_concentration_per_run,
    diffusivity,
    run_layer_stability_number,
    observed,
    slot_error_variance,
    sensor_target_site,
    patch_live_count,
):
    member_wind = run_layer_stability_number[:, :, None, None]
    extended = extended_2(starting_concentration_per_run, (("sub", 2), ("rep", 3)), STEPS)
    wide_diffusivity = extended_2(diffusivity, (("sub", 0), ("rep", 1)), STEPS)
    row_count = starting_concentration_per_run.shape[2]
    column_count = starting_concentration_per_run.shape[3]
    global_rows = lax.axis_index("sub") * row_count - STEPS + jnp.arange(row_count + 2 * STEPS)
    global_columns = (
        lax.axis_index("rep") * column_count - STEPS + jnp.arange(column_count + 2 * STEPS)
    )
    rows_inside = (global_rows >= 0) & (global_rows < row_count * lax.axis_size("sub"))
    columns_inside = (global_columns >= 0) & (global_columns < column_count * lax.axis_size("rep"))
    inside_mask = (rows_inside[:, None] & columns_inside[None, :]).astype(jnp.float32)
    for stepno in range(STEPS):
        padded = jnp.pad(extended, ((0, 0), (0, 0), (1, 1), (1, 1)))
        extended = advance(padded, wide_diffusivity, member_wind) * inside_mask
    present_state = extended[:, :, STEPS : STEPS + row_count, STEPS : STEPS + column_count]
    gathered = one_axis_at_a_time(present_state, GRP, (0, 1), 2, 0)
    members, levels, row_group, row_width = gathered.shape
    patches = row_width // PATCH
    background = jnp.transpose(
        gathered.reshape(members, levels, row_group, patches, PATCH), (2, 3, 0, 1, 4)
    ).reshape(row_group * patches, members, levels * PATCH)
    slots = observed.shape[-1]
    cell_flat = sensor_target_site.reshape(-1, slots)
    selector = (cell_flat[:, :, None] == jnp.arange(levels * PATCH)[None, None, :]).astype(
        jnp.float32
    )
    sampled = jnp.einsum("pmc,psc->pms", background, selector, precision=HIGHEST)
    result = analyse(
        background,
        sampled,
        observed.reshape(-1, slots),
        slot_error_variance.reshape(-1, slots),
        patch_live_count.reshape(-1),
    )
    returned = jnp.transpose(
        result.reshape(row_group, patches, members, levels, PATCH), (2, 3, 0, 1, 4)
    ).reshape(members, levels, row_group, row_width)
    return lax.all_to_all(returned, GRP, split_axis=0, concat_axis=2, tiled=True)


def solution(mesh):
    split = Mesh(
        mesh.devices.reshape(16, 4, mesh.shape["sub"], mesh.shape["rep"]),
        ("grp_0", "grp_1", "sub", "rep"),
    )
    return jax.shard_map(
        on_device,
        mesh=split,
        in_specs=(
            P(GRP, None, "sub", "rep"),
            P("sub", "rep"),
            P(GRP, None),
            P(SUB_GRP, "rep", None),
            P(SUB_GRP, "rep", None),
            P(SUB_GRP, "rep", None),
            P(SUB_GRP, "rep"),
        ),
        out_specs=P(GRP, None, "sub", "rep"),
        check_vma=False,
    )
```

profile of v0, /device:TPU:24, one launch (start us, length us, event | category | flops | bytes accessed | tf_op | source)
XLA Modules:
  0.0 158.4 jit_solution(5340521489498884608)
XLA Ops:
  0.0 0.8 fusion.72
  0.8 1.3 collective-permute-start.4
  2.1 4.5 %collective-permute-start.5 = (f32[4,256]{1,0:T(4,128)S(1)}, f32[4,256]{1,0:T(4,128)S(1)}, u32[]{:S(2)}, u32[]{:S(2)}) collective-permute-start(f32[4,256]{1,0:T(4,128)S(1)} %get-tuple-element.17), channel_id=1, source_target_pairs={{2,0},{4,2},{6,4},{3,1},{5,3},{7,5},{10,8},{12,10},{14,12},{11,9},... | collective-permute-start | bytes 12296 | tf_op jit(solution)/shard_map/ppermute | solution.py:25
  6.6 0.9 fusion.70
  7.5 1.3 collective-permute-start
  8.8 4.5 %collective-permute-start.1 = (f32[1,8,4,256]{3,2,1,0:T(4,128)S(1)}, f32[1,8,4,256]{3,2,1,0:T(4,128)S(1)}, u32[]{:S(2)}, u32[]{:S(2)}) collective-permute-start(f32[1,8,4,256]{3,2,1,0:T(4,128)S(1)} %get-tuple-element.11), channel_id=1, source_target_pairs={{2,0},{4,2},{6,4},{3,1},{5,3},{7,5},{10,8},{12,10},{14,12},{11,9},... | collective-permute-start | bytes 98312 | tf_op jit(solution)/shard_map/ppermute | solution.py:25
  13.6 0.9 pad_maximum_fusion.3
  14.5 1.3 collective-permute-start.6
  15.8 1.3 collective-permute-start.7
  17.4 3.0 %collective-permute-start.2 = (f32[1,8,72,4]{3,2,1,0:T(8,128)S(1)}, f32[1,8,72,4]{3,2,1,0:T(8,128)S(1)}, u32[]{:S(2)}, u32[]{:S(2)}) collective-permute-start(f32[1,8,72,4]{3,2,1,0:T(8,128)S(1)} %get-tuple-element.8), channel_id=1, source_target_pairs={{0,1},{2,3},{4,5},{6,7},{8,9},{10,11},{12,13},{14,15},{16,17},{18,... | collective-permute-start | bytes 27656 | tf_op jit(solution)/shard_map/ppermute | solution.py:24
  20.4 1.3 collective-permute-start.3
  22.0 1.9 %collective-permute-done.3 = f32[1,8,72,4]{3,2,1,0:T(8,128)S(1)} collective-permute-done((f32[1,8,72,4]{3,2,1,0:T(8,128)S(1)}, f32[1,8,72,4]{3,2,1,0:T(8,128)S(1)}, u32[]{:S(2)}, u32[]{:S(2)}) %collective-permute-start.3) | collective-permute-done | bytes 9248 | tf_op jit(solution)/shard_map/ppermute | solution.py:25
  27.0 0.8 fusion.30
  28.6 1.1 copy.22
  29.7 15.2 %all-to-all-start = ((f32[16,4,1,8,1,256]{5,3,1,4,2,0:T(8,128)}), f32[16,4,1,8,1,256]{5,3,1,4,2,0:T(8,128)S(1)}, u32[]{:S(2)}, u32[]{:S(2)}) async-start(f32[16,4,1,8,1,256]{5,3,1,4,2,0:T(8,128)} %bitcast.3), calls=%async_computation | async-start | bytes 1048576 | tf_op jit(solution)/shard_map/all_to_all | solution.py:46
  44.9 29.2 %all-to-all-done = f32[16,4,1,8,1,256]{5,3,1,4,2,0:T(8,128)S(1)} async-done(((f32[16,4,1,8,1,256]{5,3,1,4,2,0:T(8,128)}), f32[16,4,1,8,1,256]{5,3,1,4,2,0:T(8,128)S(1)}, u32[]{:S(2)}, u32[]{:S(2)}) %all-to-all-start) | async-done | bytes 524320 | tf_op jit(solution)/shard_map/all_to_all | solution.py:46
  74.1 0.8 copy.23
  75.0 4.3 %all-to-all-start.1 = ((f32[16,4,1,8,1,256]{5,3,0,4,2,1:T(8,128)}), f32[16,4,1,8,1,256]{5,3,0,4,2,1:T(8,128)S(1)}, u32[]{:S(2)}, u32[]{:S(2)}) async-start(f32[16,4,1,8,1,256]{5,3,0,4,2,1:T(8,128)} %copy.23), calls=%async_computation.1 | async-start | bytes 1048576 | tf_op jit(solution)/shard_map/all_to_all | solution.py:46
  79.3 8.0 %all-to-all-done.1 = f32[16,4,1,8,1,256]{5,3,0,4,2,1:T(8,128)S(1)} async-done(((f32[16,4,1,8,1,256]{5,3,0,4,2,1:T(8,128)}), f32[16,4,1,8,1,256]{5,3,0,4,2,1:T(8,128)S(1)}, u32[]{:S(2)}, u32[]{:S(2)}) %all-to-all-start.1) | async-done | bytes 524320 | tf_op jit(solution)/shard_map/all_to_all | solution.py:46
  88.4 0.9 fusion.73
  92.4 11.7 %custom-call.9 = f32[2,64,64]{2,1,0:T(8,128)S(1)} custom-call(f32[2,64,64]{2,1,0:T(8,128)S(1)} %get-tuple-element.12), custom_call_target="Cholesky" | custom-call | tf_op jit(solution)/shard_map/jit(cholesky)/cholesky | solution.py:82
  104.4 9.8 %custom-call.10 = f32[2,1,64,64]{2,3,1,0:T(8,128)S(1)} custom-call(f32[2,1,64,64]{3,2,1,0:T(8,128)S(1)} %select_bitcast_fusion), custom_call_target="InvertDiagBlocksLowerTriangular" | custom-call | tf_op jit(solution)/shard_map/triangular_solve | solution.py:86
  116.2 41.2 %all_to_all.28 = f32[64,8,1,256]{3,1,2,0:T(8,128)S(1)} all-to-all(f32[64,8,1,256]{3,1,2,0:T(8,128)S(1)} %bitcast.96), channel_id=1, replica_groups=mesh['grp_0'=16,'grp_1'=4,'sub'=4,'rep'=2] {'grp_0','grp_1'}, dimensions={0} | all-to-all | bytes 1048576 | tf_op jit(solution)/shard_map/all_to_all | solution.py:150
  157.4 1.0 copy.29
  (70 shorter events, 10.8 us)
Async XLA Ops:
  0.0 17.1 %copy-start = (f32[1,8,64,256]{3,2,1,0:T(8,128)S(1)}, f32[1,8,64,256]{3,2,1,0:T(8,128)}, u32[]{:S(2)}) copy-start(f32[1,8,64,256]{3,2,1,0:T(8,128)} %param.7) | copy-start | bytes 1572868
  0.8 12.8 %collective-permute-start.4 = (f32[4,256]{1,0:T(4,128)S(1)}, f32[4,256]{1,0:T(4,128)S(1)}, u32[]{:S(2)}, u32[]{:S(2)}) collective-permute-start(f32[4,256]{1,0:T(4,128)S(1)} %get-tuple-element.16), channel_id=1, source_target_pairs={{0,2},{2,4},{4,6},{1,3},{3,5},{5,7},{8,10},{10,12},{12,14},{9,11},... | collective-permute-start | bytes 12296 | tf_op jit(solution)/shard_map/ppermute | solution.py:24
  2.1 11.5 %collective-permute-start.5 = (f32[4,256]{1,0:T(4,128)S(1)}, f32[4,256]{1,0:T(4,128)S(1)}, u32[]{:S(2)}, u32[]{:S(2)}) collective-permute-start(f32[4,256]{1,0:T(4,128)S(1)} %get-tuple-element.17), channel_id=1, source_target_pairs={{2,0},{4,2},{6,4},{3,1},{5,3},{7,5},{10,8},{12,10},{14,12},{11,9},... | collective-permute-start | bytes 12296 | tf_op jit(solution)/shard_map/ppermute | solution.py:25
  7.5 9.6 %collective-permute-start = (f32[1,8,4,256]{3,2,1,0:T(4,128)S(1)}, f32[1,8,4,256]{3,2,1,0:T(4,128)S(1)}, u32[]{:S(2)}, u32[]{:S(2)}) collective-permute-start(f32[1,8,4,256]{3,2,1,0:T(4,128)S(1)} %get-tuple-element.10), channel_id=1, source_target_pairs={{0,2},{2,4},{4,6},{1,3},{3,5},{5,7},{8,10},{10,12},{12,14},{9,11},... | collective-permute-start | bytes 98312 | tf_op jit(solution)/shard_map/ppermute | solution.py:24
  8.8 8.3 %collective-permute-start.1 = (f32[1,8,4,256]{3,2,1,0:T(4,128)S(1)}, f32[1,8,4,256]{3,2,1,0:T(4,128)S(1)}, u32[]{:S(2)}, u32[]{:S(2)}) collective-permute-start(f32[1,8,4,256]{3,2,1,0:T(4,128)S(1)} %get-tuple-element.11), channel_id=1, source_target_pairs={{2,0},{4,2},{6,4},{3,1},{5,3},{7,5},{10,8},{12,10},{14,12},{11,9},... | collective-permute-start | bytes 98312 | tf_op jit(solution)/shard_map/ppermute | solution.py:25
  14.5 7.2 %collective-permute-start.6 = (f32[72,4]{1,0:T(8,128)S(1)}, f32[72,4]{1,0:T(8,128)S(1)}, u32[]{:S(2)}, u32[]{:S(2)}) collective-permute-start(f32[72,4]{1,0:T(8,128)S(1)} %get-tuple-element.14), channel_id=1, source_target_pairs={{0,1},{2,3},{4,5},{6,7},{8,9},{10,11},{12,13},{14,15},{16,17},{18,... | collective-permute-start | bytes 3464 | tf_op jit(solution)/shard_map/ppermute | solution.py:24
  15.8 5.9 %collective-permute-start.7 = (f32[72,4]{1,0:T(8,128)S(1)}, f32[72,4]{1,0:T(8,128)S(1)}, u32[]{:S(2)}, u32[]{:S(2)}) collective-permute-start(f32[72,4]{1,0:T(8,128)S(1)} %get-tuple-element.15), channel_id=1, source_target_pairs={{1,0},{3,2},{5,4},{7,6},{9,8},{11,10},{13,12},{15,14},{17,16},{19,... | collective-permute-start | bytes 3464 | tf_op jit(solution)/shard_map/ppermute | solution.py:25
  17.2 4.5 %copy-start.1 = (f32[64,256]{1,0:T(8,128)S(1)}, f32[64,256]{1,0:T(8,128)}, u32[]{:S(2)}) copy-start(f32[64,256]{1,0:T(8,128)} %param.8) | copy-start | bytes 196612
  17.4 4.6 %collective-permute-start.2 = (f32[1,8,72,4]{3,2,1,0:T(8,128)S(1)}, f32[1,8,72,4]{3,2,1,0:T(8,128)S(1)}, u32[]{:S(2)}, u32[]{:S(2)}) collective-permute-start(f32[1,8,72,4]{3,2,1,0:T(8,128)S(1)} %get-tuple-element.8), channel_id=1, source_target_pairs={{0,1},{2,3},{4,5},{6,7},{8,9},{10,11},{12,13},{14,15},{16,17},{18,... | collective-permute-start | bytes 27656 | tf_op jit(solution)/shard_map/ppermute | solution.py:24
  20.4 3.5 %collective-permute-start.3 = (f32[1,8,72,4]{3,2,1,0:T(8,128)S(1)}, f32[1,8,72,4]{3,2,1,0:T(8,128)S(1)}, u32[]{:S(2)}, u32[]{:S(2)}) collective-permute-start(f32[1,8,72,4]{3,2,1,0:T(8,128)S(1)} %get-tuple-element.9), channel_id=1, source_target_pairs={{1,0},{3,2},{5,4},{7,6},{9,8},{11,10},{13,12},{15,14},{17,16},{19,... | collective-permute-start | bytes 27656 | tf_op jit(solution)/shard_map/ppermute | solution.py:25
  24.4 0.7 copy-start.2
  29.7 44.5 %all-to-all-start = ((f32[16,4,1,8,1,256]{5,3,1,4,2,0:T(8,128)}), f32[16,4,1,8,1,256]{5,3,1,4,2,0:T(8,128)S(1)}, u32[]{:S(2)}, u32[]{:S(2)}) async-start(f32[16,4,1,8,1,256]{5,3,1,4,2,0:T(8,128)} %bitcast.3), calls=%async_computation | async-start | bytes 1048576 | tf_op jit(solution)/shard_map/all_to_all | solution.py:46
  75.0 12.4 %all-to-all-start.1 = ((f32[16,4,1,8,1,256]{5,3,0,4,2,1:T(8,128)}), f32[16,4,1,8,1,256]{5,3,0,4,2,1:T(8,128)S(1)}, u32[]{:S(2)}, u32[]{:S(2)}) async-start(f32[16,4,1,8,1,256]{5,3,0,4,2,1:T(8,128)} %copy.23), calls=%async_computation.1 | async-start | bytes 1048576 | tf_op jit(solution)/shard_map/all_to_all | solution.py:46
  87.7 0.7 copy-start.3
  88.4 0.9 copy-start.5
  89.3 0.7 copy-start.4
  89.3 0.7 copy-start.6
where the time goes:
time: 159 us; the launch traced here: 158 us
  blocking collectives  41.2 us (26%)
  waiting for transfers between devices  39.2 us (25%)
  starting transfers between devices  38.1 us (24%)
  other arithmetic  27.2 us (17%)
  local copies, waits for them, and re-layouts  7.49 us (5%)
  matrix products  4.71 us (3%)
    all_to_all x1, blocking collectives, on_device(): lax.all_to_all(returned, GRP, split_axis=0, concat_axis=2, tiled=True)  41.2 us
    all_to_all x2, waiting for transfers between devices, moved_by_axis(): lax.all_to_all(parts, axes[k], split_axis=k, concat_axis=k, tiled=True)  37.3 us
    all_to_all x2, starting transfers between devices, moved_by_axis(): lax.all_to_all(parts, axes[k], split_axis=k, concat_axis=k, tiled=True)  19.5 us
    another operation x3, other arithmetic, analyse(): factor = jnp.linalg.cholesky(system)  11.9 us
    ppermute x4, starting transfers between devices, extended_2(): after = lax.ppermute(initial, axis, down)  11.7 us
    another operation x3, other arithmetic, analyse(): lax.linalg.triangular_solve(factor, halfway, left_side=True, lower=True,...  9.92 us
    ppermute x4, starting transfers between devices, extended_2(): before = lax.ppermute(last, axis, up)  6.9 us
  transfers between devices with their start and end apart: 10, of which 3 were waited for; matrix products, arithmetic and copies ran while one was open for 2% of the time, Pallas kernels for 0%

commit v1 on v0

v1 whole, which is shorter than its diff:
```python
import jax
import jax.numpy as jnp
from jax import lax
from jax.experimental import pallas as pl
from jax.experimental.pallas import tpu as pltpu
from jax.sharding import Mesh
from jax.sharding import PartitionSpec as P

LEVELS = 8
PATCH = 128
STEPS = 4
NS_ITERS = 4
MEMBERS = 64
ROWS = 64
COLS = 256
TALL = ROWS + 2 * STEPS
GRP = ("grp_0", "grp_1")
SUB_GRP = ("sub", "grp_0", "grp_1")
HIGHEST = lax.Precision.HIGHEST
VMEM_LIMIT = 24 * 1024 * 1024


def pack_kernel(rep_ref, x_ref, d_ref, first_ref, last_ref, side_ref):
    for h in range(2):
        cols = slice(h * PATCH, (h + 1) * PATCH)
        for l in range(LEVELS):
            top = x_ref[ROWS * l : ROWS * l + 8, cols]
            end = x_ref[ROWS * l + ROWS - 8 : ROWS * l + ROWS, cols]
            first_ref[pl.ds(8 * h + l, STEPS, stride=16), :] = top[:STEPS]
            last_ref[pl.ds(8 * h + l, STEPS, stride=16), :] = end[8 - STEPS :]
        first_ref[64 + 8 * h : 72 + 8 * h, :] = d_ref[0:8, cols]
        last_ref[64 + 8 * h : 72 + 8 * h, :] = d_ref[ROWS - 8 : ROWS, cols]
    half = pl.ds(pl.multiple_of((1 - rep_ref[0]) * PATCH, PATCH), PATCH)
    side_ref[0 : LEVELS * ROWS, :] = x_ref[:, half]
    side_ref[LEVELS * ROWS :, :] = d_ref[:, half]


def forecast_kernel(rep_ref, x_ref, d_ref, below_ref, above_ref, side_ref, corner_ref, wind_ref, out_ref, a_ref, b_ref, w_ref):
    rep = rep_ref[0]
    lane = lax.broadcasted_iota(jnp.int32, (8, PATCH), 1)
    low = jnp.where(rep == 0, 0, PATCH - STEPS)
    keep = (lane >= low) & (lane < low + STEPS)
    keep_rows = jnp.broadcast_to(keep[:1], (ROWS, PATCH))
    for l in range(LEVELS):
        for t in range(2):
            a_ref[pl.ds(24 * STEPS + 8 * t + l, ROWS, stride=24), :] = x_ref[
                ROWS * l : ROWS * (l + 1), t * PATCH : (t + 1) * PATCH
            ]
        a_ref[pl.ds(24 * STEPS + 16 + l, ROWS, stride=24), :] = jnp.where(
            keep_rows, side_ref[ROWS * l : ROWS * (l + 1), :], 0.0
        )
    for ref, base, corner in ((above_ref, 0, 40), (below_ref, STEPS + ROWS, 0)):
        for r in range(STEPS):
            at = 24 * (base + r)
            a_ref[at : at + 16, :] = ref[16 * r : 16 * r + 16, :]
            a_ref[at + 16 : at + 24, :] = jnp.where(
                keep, corner_ref[corner + 8 * r : corner + 8 * r + 8, :], 0.0
            )
    for t in range(2):
        w_ref[80 * t + 8 : 80 * t + 8 + ROWS, :] = d_ref[:, t * PATCH : (t + 1) * PATCH]
    w_ref[168 : 168 + ROWS, :] = jnp.where(keep_rows, side_ref[LEVELS * ROWS :, :], 0.0)
    for ref, base, corner in ((above_ref, 0, 72), (below_ref, 8 + ROWS, 32)):
        for t in range(2):
            w_ref[80 * t + base : 80 * t + base + 8, :] = ref[64 + 8 * t : 72 + 8 * t, :]
        w_ref[160 + base : 168 + base, :] = jnp.where(keep, corner_ref[corner : corner + 8, :], 0.0)
    wind = wind_ref[...]
    winds = [wind, wind, jnp.where(keep, wind, 0.0)]
    first_lane, last_lane = lane == 0, lane == PATCH - 1

    def tiles(ref, row):
        return [ref[pl.ds(pl.multiple_of(24 * row + 8 * t, 8), 8), :] for t in range(3)]

    for step in range(STEPS):
        src, dst = (a_ref, b_ref) if step % 2 == 0 else (b_ref, a_ref)

        def body(row, carry, src=src, dst=dst, step=step):
            northern, centre = carry
            southern = tiles(src, row + 1)
            right = [pltpu.roll(v, 1, 1) for v in centre]
            left = [pltpu.roll(v, PATCH - 1, 1) for v in centre]
            for t in range(3 if step < STEPS - 1 else 2):
                west = jnp.where(first_lane, right[(t + 2) % 3], right[t])
                east = jnp.where(last_lane, left[(t + 1) % 3], left[t])
                spread = northern[t] + southern[t] + (west + east) - 4.0 * centre[t]
                d_row = w_ref[pl.ds(80 * t + row + STEPS, 1), :]
                new = centre[t] + d_row * spread - winds[t] * (centre[t] - west)
                if step < STEPS - 1:
                    dst[pl.ds(pl.multiple_of(24 * row + 8 * t, 8), 8), :] = new
                else:
                    at = pl.multiple_of(16 * (row - STEPS) + 8 * t, 8)
                    out_ref[pl.ds(at, 8), :] = new
            return centre, southern

        first = step + 1
        lax.fori_loop(
            first, TALL - first, body, (tiles(src, first - 1), tiles(src, first)), unroll=2
        )


def analysis_kernel(count_ref, x_ref, obs_ref, var_ref, site_ref, out_ref, pert_ref):
    members = MEMBERS
    lanes = lax.broadcasted_iota(jnp.int32, (8, PATCH), 1)
    site = site_ref[...]
    level = site // PATCH
    column = site - level * PATCH
    means = [[None] * LEVELS for _ in range(2)]
    sampled = []
    for p in range(2):
        pick = jnp.broadcast_to(column[p : p + 1, :], (members, PATCH))
        got = jnp.zeros((members, PATCH), jnp.float32)
        for l in range(LEVELS):
            block = x_ref[pl.ds(8 * p + l, members, stride=16), :]
            mean = jnp.sum(block, axis=0, keepdims=True) * (1.0 / members)
            means[p][l] = mean
            pert_ref[p * members : (p + 1) * members, l * PATCH : (l + 1) * PATCH] = block - mean
            here = jnp.take_along_axis(block, pick, axis=1, mode="promise_in_bounds")
            got = jnp.where(level[p : p + 1, :] == l, here, got)
        sampled.append(got)
    perts, weighteds, forcings = [], [], []
    for p in range(2):
        got = sampled[p]
        mean = jnp.sum(got, axis=0, keepdims=True) * (1.0 / members)
        pert = got - mean
        live = lanes[:1] < count_ref[p]
        precision = jnp.where(live, 1.0 / var_ref[p : p + 1, :], 0.0)
        weighted = pert * precision
        innovation = obs_ref[p : p + 1, :] - mean
        perts.append(pert)
        weighteds.append(weighted)
        forcings.append(jnp.sum(weighted * innovation, axis=1, keepdims=True))
    nt = (((1,), (1,)), ((), ()))
    both = 2 * members
    cross = lax.dot_general(
        jnp.concatenate(weighteds, 0), jnp.concatenate(perts, 0), nt,
        precision=HIGHEST, preferred_element_type=jnp.float32,
    )
    row_id = lax.broadcasted_iota(jnp.int32, (both, both), 0)
    col_id = lax.broadcasted_iota(jnp.int32, (both, both), 1)
    eye = (row_id == col_id).astype(jnp.float32)
    system = jnp.where((row_id < members) == (col_id < members), cross, 0.0) + (members - 1.0) * eye

    m = system[:members, :] + system[members:, :]
    left = lanes < members
    m = [m[8 * q : 8 * q + 8, :] for q in range(8)]
    f = [
        jnp.where(left, forcings[0][8 * q : 8 * q + 8, :], forcings[1][8 * q : 8 * q + 8, :])
        for q in range(8)
    ]
    sub_id = lax.broadcasted_iota(jnp.int32, (8, PATCH), 0)
    inverse = [jnp.zeros((8, PATCH), jnp.float32) for _ in range(8)]
    for k in range(members):
        kq, kr = divmod(k, 8)
        at = jnp.where(left, k, members + k)
        column_k = [jnp.take_along_axis(v, at, axis=1, mode="promise_in_bounds") for v in m]
        inv = 1.0 / column_k[kq][kr : kr + 1, :]
        row_k = m[kq][kr : kr + 1, :] * inv
        f_k = f[kq][kr : kr + 1, :] * inv
        here = sub_id == kr
        inverse[kq] = jnp.where(here, inv, inverse[kq])
        column_k[kq] = jnp.where(here, 0.0, column_k[kq])
        m = [v - c * row_k for v, c in zip(m, column_k)]
        f = [v - c * f_k for v, c in zip(f, column_k)]
    weight = jnp.concatenate([v * i for v, i in zip(f, inverse)], 0)

    squares = jnp.sum(system * system, axis=1, keepdims=True)
    norms = [
        jnp.sqrt(jnp.sum(squares[p * members : (p + 1) * members], axis=0, keepdims=True))
        for p in range(2)
    ]
    norm = jnp.where(row_id[:, :1] < members, norms[0], norms[1])

    def mm(a, b):
        return jnp.dot(a, b, precision=HIGHEST, preferred_element_type=jnp.float32)

    iterate = system / norm
    root = None
    for sweep in range(NS_ITERS):
        update = 1.5 * eye - 0.5 * (iterate if root is None else mm(root, iterate))
        if sweep < NS_ITERS - 1:
            iterate = mm(iterate, update)
        root = update if root is None else mm(update, root)
    spread = root * jnp.sqrt((members - 1.0) / norm)
    zero = jnp.zeros((members, PATCH), jnp.float32)
    left_all = col_id[:members] < members
    combined = spread + jnp.concatenate(
        [jnp.where(left_all, weight, zero), jnp.where(left_all, zero, weight)], 0
    )
    tn = (((0,), (0,)), ((), ()))
    for l in range(LEVELS):
        moved = lax.dot_general(
            combined, pert_ref[:, l * PATCH : (l + 1) * PATCH], tn,
            precision=HIGHEST, preferred_element_type=jnp.float32,
        )
        for p in range(2):
            out_ref[pl.ds(8 * p + l, members, stride=16), :] = (
                moved[p * members : (p + 1) * members] + means[p][l]
            )


def unpack_kernel(x_ref, out_ref):
    for l in range(LEVELS):
        for h in range(2):
            out_ref[ROWS * l : ROWS * (l + 1), h * PATCH : (h + 1) * PATCH] = x_ref[
                pl.ds(8 * h + l, ROWS, stride=16), :
            ]


VMEM = pl.BlockSpec(memory_space=pltpu.VMEM)
SMEM = pl.BlockSpec(memory_space=pltpu.SMEM)


def call(kernel, outs, specs, scratch=(), flops=1_000_000, name=None):
    shapes = [jax.ShapeDtypeStruct(s, jnp.float32) for s in outs]
    return pl.pallas_call(
        kernel,
        out_shape=shapes if len(shapes) > 1 else shapes[0],
        in_specs=specs,
        out_specs=[VMEM] * len(shapes) if len(shapes) > 1 else VMEM,
        scratch_shapes=[pltpu.VMEM(s, jnp.float32) for s in scratch],
        compiler_params=pltpu.CompilerParams(vmem_limit_bytes=VMEM_LIMIT),
        cost_estimate=pl.CostEstimate(flops=flops, bytes_accessed=1_000_000, transcendentals=0),
        name=name,
    )


def on_device(start, diffusivity, stability, observed, variance, site, live):
    rep = lax.axis_index("rep").astype(jnp.int32).reshape(1)
    x = start.reshape(LEVELS * ROWS, COLS)
    first, last, side = call(
        pack_kernel,
        [(80, PATCH), (80, PATCH), ((LEVELS + 1) * ROWS, PATCH)],
        [SMEM, VMEM, VMEM],
        name="pack",
    )(rep, x, diffusivity)
    n = lax.axis_size("sub")
    below = lax.ppermute(first, "sub", [(i + 1, i) for i in range(n - 1)])
    above = lax.ppermute(last, "sub", [(i, i + 1) for i in range(n - 1)])
    swap = [(0, 1), (1, 0)]
    side = lax.ppermute(side, "rep", swap)
    ends = jnp.concatenate([below, above], axis=0).reshape(10, 2, 8, PATCH)
    corner = lax.dynamic_index_in_dim(ends, 1 - rep[0], axis=1, keepdims=False)
    corner = lax.ppermute(corner.reshape(80, PATCH), "rep", swap)
    wind = jnp.broadcast_to(stability.reshape(LEVELS, 1), (LEVELS, PATCH))
    forecast = call(
        forecast_kernel,
        [(ROWS * 16, PATCH)],
        [SMEM] + [VMEM] * 7,
        scratch=[(TALL * 24, PATCH), (TALL * 24, PATCH), (3 * (ROWS + 16), PATCH)],
        name="forecast",
    )(rep, x, diffusivity, below, above, side, corner, wind)
    gathered = lax.all_to_all(forecast.reshape(ROWS, 16, PATCH), GRP, 0, 0, tiled=True)
    analysed = call(
        analysis_kernel,
        [(MEMBERS * 16, PATCH)],
        [SMEM] + [VMEM] * 4,
        scratch=[(2 * MEMBERS, LEVELS * PATCH)],
        name="analysis",
    )(
        live.reshape(2),
        gathered.reshape(MEMBERS * 16, PATCH),
        observed.reshape(2, PATCH),
        variance.reshape(2, PATCH),
        site.reshape(2, PATCH),
    )
    returned = lax.all_to_all(analysed.reshape(MEMBERS, 16, PATCH), GRP, 0, 0, tiled=True)
    out = call(unpack_kernel, [(LEVELS * ROWS, COLS)], [VMEM], name="unpack")(
        returned.reshape(ROWS * 16, PATCH)
    )
    return out.reshape(1, LEVELS, ROWS, COLS)


def solution(mesh):
    split = Mesh(
        mesh.devices.reshape(16, 4, mesh.shape["sub"], mesh.shape["rep"]),
        ("grp_0", "grp_1", "sub", "rep"),
    )
    return jax.shard_map(
        on_device,
        mesh=split,
        in_specs=(
            P(GRP, None, "sub", "rep"),
            P("sub", "rep"),
            P(GRP, None),
            P(SUB_GRP, "rep", None),
            P(SUB_GRP, "rep", None),
            P(SUB_GRP, "rep", None),
            P(SUB_GRP, "rep"),
        ),
        out_specs=P(GRP, None, "sub", "rep"),
        check_vma=False,
    )
```

time: 159 us -> 125 us (0.79)
  blocking collectives: 41.2 us -> 89.5 us
  waiting for transfers between devices: 39.2 us -> 3.85 us
  starting transfers between devices: 38.1 us -> 7.91 us
  other arithmetic: 27.2 us -> 0.01 us
  Pallas kernels: 0 us -> 20.2 us
  local copies, waits for them, and re-layouts: 7.49 us -> 2.66 us
  matrix products: 4.71 us -> 0 us
    all_to_all x1 -> x2, blocking collectives: 41.2 us -> 89.5 us  [the longest x1 51.5 us: on_device(): lax.all_to_all(forecast.reshape(ROWS, 16, PATCH), GRP, 0, 0, tiled=True)]
    all_to_all x2 -> x0, waiting for transfers between devices: 37.3 us -> none  [moved_by_axis(): lax.all_to_all(parts, axes[k], split_axis=k, concat_axis=k, tiled=True)]
    another operation x6 -> x0, other arithmetic: 21.8 us -> none  [the longest x3 11.9 us: analyse(): factor = jnp.linalg.cholesky(system)]
    pallas_call x0 -> x4, Pallas kernels: none -> 20.2 us  [the longest x1 11.8 us: on_device(): call(forecast_kernel, [(ROWS * 16, PATCH)], [SMEM] + [VMEM] * 7, scratch=...]
    all_to_all x2 -> x0, starting transfers between devices: 19.5 us -> none  [moved_by_axis(): lax.all_to_all(parts, axes[k], split_axis=k, concat_axis=k, tiled=True)]
    ppermute x8 -> x4, starting transfers between devices: 18.6 us -> 7.91 us  [the longest x1 2.78 us: on_device(): below = lax.ppermute(first, 'sub', [(i + 1, i) for i in range(n - 1)])]
    dot_general x15 -> x0, matrix products: 4.33 us -> none  [the longest x1 0.87 us: on_device(): jnp.einsum('pmc,psc->pms', background, selector, precision=HIGHEST)]
    slice x6 -> x0, local copies, waits for them, and re-layouts: 2.05 us -> none  [the longest x4 1.88 us: extended_2(): last = lax.slice_in_dim(x, length - width, length, axis=dim)]
  transfers between devices with their start and end apart: 10 -> 4, of which waited for: 3 -> 2; matrix products, arithmetic and copies ran while one was open for 2% -> 0% of each run, Pallas kernels for 0% -> 0%
where the time goes in v1:
time: 125 us; the launch traced here: 124 us
  blocking collectives  89.5 us (72%)
  Pallas kernels  20.2 us (16%)
  starting transfers between devices  7.91 us (6%)
  waiting for transfers between devices  3.85 us (3%)
  local copies, waits for them, and re-layouts  2.66 us (2%)
    all_to_all x1, blocking collectives, on_device(): lax.all_to_all(forecast.reshape(ROWS, 16, PATCH), GRP, 0, 0, tiled=True)  51.5 us
    all_to_all x1, blocking collectives, on_device(): lax.all_to_all(analysed.reshape(MEMBERS, 16, PATCH), GRP, 0, 0, tiled=True)  38 us
    pallas_call x1, Pallas kernels, on_device(): call(forecast_kernel, [(ROWS * 16, PATCH)], [SMEM] + [VMEM] * 7, scratch=...  11.8 us
    pallas_call x1, Pallas kernels, on_device(): call(analysis_kernel, [(MEMBERS * 16, PATCH)], [SMEM] + [VMEM] * 4, scrat...  7.39 us
    ppermute x1, starting transfers between devices, on_device(): below = lax.ppermute(first, 'sub', [(i + 1, i) for i in range(n - 1)])  2.78 us
    ppermute x1, waiting for transfers between devices, on_device(): above = lax.ppermute(last, 'sub', [(i, i + 1) for i in range(n - 1)])  2.66 us
    unnamed x18, local copies, waits for them, and re-layouts  2.58 us
  transfers between devices with their start and end apart: 4, of which 2 were waited for; matrix products, arithmetic and copies ran while one was open for 0% of the time, Pallas kernels for 0%

profile of v1, /device:TPU:24, one launch (start us, length us, event | category | flops | bytes accessed | tf_op | source)
XLA Modules:
  0.0 124.2 jit_solution(8238055130626116683)
XLA Ops:
  0.0 1.0 copy-done
  1.0 0.8 copy-done.2
  1.9 2.8 %collective-permute-start = (f32[80,128]{1,0:T(8,128)S(1)}, f32[80,128]{1,0:T(8,128)S(1)}, u32[]{:S(2)}, u32[]{:S(2)}) collective-permute-start(f32[80,128]{1,0:T(8,128)S(1)} %get-tuple-element.8), channel_id=1, source_target_pairs={{2,0},{4,2},{6,4},{3,1},{5,3},{7,5},{10,8},{12,10},{14,12},{11,9},... | collective-permute-start | bytes 122888 | tf_op jit(solution)/shard_map/ppermute | solution.py:236
  4.7 1.3 %collective-permute-start.1 = (f32[80,128]{1,0:T(8,128)S(1)}, f32[80,128]{1,0:T(8,128)S(1)}, u32[]{:S(2)}, u32[]{:S(2)}) collective-permute-start(f32[80,128]{1,0:T(8,128)S(1)} %get-tuple-element.9), channel_id=1, source_target_pairs={{0,2},{2,4},{4,6},{1,3},{3,5},{5,7},{8,10},{10,12},{12,14},{9,11},... | collective-permute-start | bytes 122888 | tf_op jit(solution)/shard_map/ppermute | solution.py:237
  6.0 1.9 %collective-permute-start.2 = (f32[576,128]{1,0:T(8,128)S(1)}, f32[576,128]{1,0:T(8,128)S(1)}, u32[]{:S(2)}, u32[]{:S(2)}) collective-permute-start(f32[576,128]{1,0:T(8,128)S(1)} %get-tuple-element.10), channel_id=1, source_target_pairs={{0,1},{1,0},{2,3},{3,2},{4,5},{5,4},{6,7},{7,6},{8,9},{9,8},{10,11... | collective-permute-start | bytes 884744 | tf_op jit(solution)/shard_map/ppermute | solution.py:239
  7.9 0.0 collective-permute-done.below_ref
  8.0 2.7 %collective-permute-done.1.above_ref = f32[80,128]{1,0:T(8,128)S(1)} collective-permute-done((f32[80,128]{1,0:T(8,128)S(1)}, f32[80,128]{1,0:T(8,128)S(1)}, u32[]{:S(2)}, u32[]{:S(2)}) %collective-permute-start.1) | collective-permute-done | bytes 40992 | tf_op jit(solution)/shard_map/ppermute | solution.py:237
  10.7 0.0 copy-start.8
  10.7 1.9 %collective-permute-start.3 = (f32[80,128]{1,0:T(8,128)S(1)}, f32[80,128]{1,0:T(8,128)S(1)}, u32[]{:S(2)}, u32[]{:S(2)}) collective-permute-start(f32[80,128]{1,0:T(8,128)S(1)} %dynamic-slice_bitcast_fusion), channel_id=1, source_target_pairs={{0,1},{1,0},{2,3},{3,2},{4,5},{5,4},{6,7},{7,6},{8,9},{9,8},{10,11... | collective-permute-start | bytes 122888 | tf_op jit(solution)/shard_map/ppermute | solution.py:242
  12.6 1.2 collective-permute-done.3.corner_ref
  13.8 0.0 collective-permute-done.2.side_ref
  13.8 0.0 copy-done.8
  13.8 0.1 broadcast_in_dim.8.wind_ref
  13.9 0.0 copy-done.1
  13.9 0.0 copy-done.3
  13.9 11.8 %forecast.1 = f32[1024,128]{1,0:T(8,128)S(1)} custom-call(s32[1]{0:T(128)} %bitcast.1.rep_ref, f32[512,256]{1,0:T(8,128)S(1)} %bitcast.18, f32[64,256]{1,0:T(8,128)S(1)} %copy-done.3, f32[80,128]{1,0:T(8,128)S(1)} %collective-permute-done.below_ref, f32[80,128]{1,0:T(8,128)S(1)} %collective-permute-done.1.above_ref, ...), custom_call_target="tpu_custom_call" | custom-call | flops 1000000 | bytes 1000000 | tf_op jit(solution)/shard_map/forecast/pallas_call | solution.py:244
  25.7 0.0 copy-start.5
  25.7 0.0 copy-start.6
  25.7 51.5 %all_to_all.10 = f32[64,16,128]{2,1,0:T(8,128)S(1)} all-to-all(f32[64,16,128]{2,1,0:T(8,128)S(1)} %bitcast.19), channel_id=1, replica_groups=mesh['grp_0'=16,'grp_1'=4,'sub'=4,'rep'=2] {'grp_0','grp_1'}, dimensions={0} | all-to-all | bytes 1048576 | tf_op jit(solution)/shard_map/all_to_all | solution.py:251
  77.2 0.0 copy-done.5
  77.2 0.7 copy-done.4
  77.9 7.4 %analysis.1 = f32[1024,128]{1,0:T(8,128)S(1)} custom-call(s32[2]{0:T(128)S(1)} %bitcast.26, f32[1024,128]{1,0:T(8,128)S(1)} %bitcast.20, f32[2,128]{1,0:T(2,128)S(1)} %bitcast.23, f32[2,128]{1,0:T(2,128)S(1)} %bitcast.24, s32[2,128]{1,0:T(2,128)S(1)} %bitcast.25), custom_call_target="tpu_custom_call" | custom-call | flops 1000000 | bytes 1000000 | tf_op jit(solution)/shard_map/analysis/pallas_call | solution.py:252
  85.3 38.0 %all_to_all.11 = f32[64,16,128]{2,1,0:T(8,128)S(1)} all-to-all(f32[64,16,128]{2,1,0:T(8,128)S(1)} %bitcast.21), channel_id=1, replica_groups=mesh['grp_0'=16,'grp_1'=4,'sub'=4,'rep'=2] {'grp_0','grp_1'}, dimensions={0} | all-to-all | bytes 1048576 | tf_op jit(solution)/shard_map/all_to_all | solution.py:265
  123.3 1.0 unpack.1
  (11 shorter events, 0.1 us)
Async XLA Ops:
  0.0 1.0 copy-start
  1.0 0.8 copy-start.2
  1.9 12.0 %copy-start.1 = (f32[1,8,64,256]{3,2,1,0:T(8,128)S(1)}, f32[1,8,64,256]{3,2,1,0:T(8,128)}, u32[]{:S(2)}) copy-start(f32[1,8,64,256]{3,2,1,0:T(8,128)} %param.7) | copy-start | bytes 1572868
  1.9 6.0 %collective-permute-start = (f32[80,128]{1,0:T(8,128)S(1)}, f32[80,128]{1,0:T(8,128)S(1)}, u32[]{:S(2)}, u32[]{:S(2)}) collective-permute-start(f32[80,128]{1,0:T(8,128)S(1)} %get-tuple-element.8), channel_id=1, source_target_pairs={{2,0},{4,2},{6,4},{3,1},{5,3},{7,5},{10,8},{12,10},{14,12},{11,9},... | collective-permute-start | bytes 122888 | tf_op jit(solution)/shard_map/ppermute | solution.py:236
  4.7 5.9 %collective-permute-start.1 = (f32[80,128]{1,0:T(8,128)S(1)}, f32[80,128]{1,0:T(8,128)S(1)}, u32[]{:S(2)}, u32[]{:S(2)}) collective-permute-start(f32[80,128]{1,0:T(8,128)S(1)} %get-tuple-element.9), channel_id=1, source_target_pairs={{0,2},{2,4},{4,6},{1,3},{3,5},{5,7},{8,10},{10,12},{12,14},{9,11},... | collective-permute-start | bytes 122888 | tf_op jit(solution)/shard_map/ppermute | solution.py:237
  6.0 7.8 %collective-permute-start.2 = (f32[576,128]{1,0:T(8,128)S(1)}, f32[576,128]{1,0:T(8,128)S(1)}, u32[]{:S(2)}, u32[]{:S(2)}) collective-permute-start(f32[576,128]{1,0:T(8,128)S(1)} %get-tuple-element.10), channel_id=1, source_target_pairs={{0,1},{1,0},{2,3},{3,2},{4,5},{5,4},{6,7},{7,6},{8,9},{9,8},{10,11... | collective-permute-start | bytes 884744 | tf_op jit(solution)/shard_map/ppermute | solution.py:239
  10.6 3.2 %copy-start.3 = (f32[64,256]{1,0:T(8,128)S(1)}, f32[64,256]{1,0:T(8,128)}, u32[]{:S(2)}) copy-start(f32[64,256]{1,0:T(8,128)} %d_ref.3) | copy-start | bytes 196612
  10.7 3.1 %copy-start.8 = (f32[1,8]{1,0:T(1,128)S(1)}, f32[1,8]{1,0:T(1,128)}, u32[]{:S(2)}) copy-start(f32[1,8]{1,0:T(1,128)} %param.9) | copy-start | bytes 100
  10.7 3.1 %collective-permute-start.3 = (f32[80,128]{1,0:T(8,128)S(1)}, f32[80,128]{1,0:T(8,128)S(1)}, u32[]{:S(2)}, u32[]{:S(2)}) collective-permute-start(f32[80,128]{1,0:T(8,128)S(1)} %dynamic-slice_bitcast_fusion), channel_id=1, source_target_pairs={{0,1},{1,0},{2,3},{3,2},{4,5},{5,4},{6,7},{7,6},{8,9},{9,8},{10,11... | collective-permute-start | bytes 122888 | tf_op jit(solution)/shard_map/ppermute | solution.py:242
  25.7 51.5 %copy-start.5 = (f32[1,2,128]{2,1,0:T(2,128)S(1)}, f32[1,2,128]{2,1,0:T(2,128)}, u32[]{:S(2)}) copy-start(f32[1,2,128]{2,1,0:T(2,128)} %param.11) | copy-start | bytes 3076
  25.7 51.5 %copy-start.6 = (s32[1,2,128]{2,1,0:T(2,128)S(1)}, s32[1,2,128]{2,1,0:T(2,128)}, u32[]{:S(2)}) copy-start(s32[1,2,128]{2,1,0:T(2,128)} %param.12) | copy-start | bytes 3076
  77.2 0.7 copy-start.4
  77.2 0.7 copy-start.7

commit v2 on v1

v2 whole, which is shorter than its diff:
```python
import jax
import jax.numpy as jnp
from jax import lax
from jax.experimental import pallas as pl
from jax.experimental.pallas import tpu as pltpu
from jax.sharding import Mesh
from jax.sharding import PartitionSpec as P

LEVELS = 8
PATCH = 128
STEPS = 4
NS_ITERS = 4
MEMBERS = 64
ROWS = 64
COLS = 256
TALL = ROWS + 2 * STEPS
GRP = ("grp_0", "grp_1")
SUB_GRP = ("sub", "grp_0", "grp_1")
HIGHEST = lax.Precision.HIGHEST
VMEM_LIMIT = 24 * 1024 * 1024


def pack_kernel(rep_ref, x_ref, d_ref, first_ref, last_ref, side_ref, top_ref, end_ref, dtop_ref, dend_ref, sems):
    half = pl.ds(pl.multiple_of((1 - rep_ref[0]) * PATCH, PATCH), PATCH)
    copies = [
        pltpu.make_async_copy(src, dst, sems.at[i])
        for i, (src, dst) in enumerate(
            (
                (x_ref.at[:, pl.ds(0, 8), :], top_ref),
                (x_ref.at[:, pl.ds(ROWS - 8, 8), :], end_ref),
                (d_ref.at[pl.ds(0, 8), :], dtop_ref),
                (d_ref.at[pl.ds(ROWS - 8, 8), :], dend_ref),
                (x_ref.at[:, :, half], side_ref.at[pl.ds(0, LEVELS)]),
                (d_ref.at[:, half], side_ref.at[LEVELS]),
            )
        )
    ]
    for copy in copies:
        copy.start()
    for copy in copies[:4]:
        copy.wait()
    for h in range(2):
        cols = slice(h * PATCH, (h + 1) * PATCH)
        for l in range(LEVELS):
            first_ref[pl.ds(8 * h + l, STEPS, stride=16), :] = top_ref[l, :STEPS, cols]
            last_ref[pl.ds(8 * h + l, STEPS, stride=16), :] = end_ref[l, 8 - STEPS :, cols]
        first_ref[64 + 8 * h : 72 + 8 * h, :] = dtop_ref[:, cols]
        last_ref[64 + 8 * h : 72 + 8 * h, :] = dend_ref[:, cols]
    for copy in copies[4:]:
        copy.wait()


def forecast_kernel(
    rep_ref, count_ref, x_ref, d_ref, below_ref, above_ref, side_ref, corner_ref, wind_ref, obs_hbm, var_hbm, site_hbm,
    out_ref, obs_out, precision_out, site_out, a_ref, b_ref, w_ref, var_ref, sems,
):
    copies = [
        pltpu.make_async_copy(src, dst, sems.at[i])
        for i, (src, dst) in enumerate(
            ((obs_hbm, obs_out), (var_hbm, var_ref), (site_hbm, site_out))
        )
    ]
    for copy in copies:
        copy.start()
    rep = rep_ref[0]
    lane = lax.broadcasted_iota(jnp.int32, (8, PATCH), 1)
    low = jnp.where(rep == 0, 0, PATCH - STEPS)
    keep = (lane >= low) & (lane < low + STEPS)
    keep_rows = jnp.broadcast_to(keep[:1], (ROWS, PATCH))
    zero = jnp.zeros((8, PATCH), jnp.float32)
    own = 24 * (STEPS + 1)
    for l in range(LEVELS):
        for t in range(2):
            a_ref[pl.ds(own + 8 * t + l, ROWS, stride=24), :] = x_ref[
                ROWS * l : ROWS * (l + 1), t * PATCH : (t + 1) * PATCH
            ]
        a_ref[pl.ds(own + 16 + l, ROWS, stride=24), :] = jnp.where(
            keep_rows, side_ref[ROWS * l : ROWS * (l + 1), :], 0.0
        )
    for ref, base, corner in ((above_ref, 1, 40), (below_ref, 1 + STEPS + ROWS, 0)):
        for r in range(STEPS):
            at = 24 * (base + r)
            a_ref[at : at + 16, :] = ref[16 * r : 16 * r + 16, :]
            a_ref[at + 16 : at + 24, :] = jnp.where(
                keep, corner_ref[corner + 8 * r : corner + 8 * r + 8, :], 0.0
            )
    for ref in (a_ref, b_ref):
        for at in (0, 24 * (TALL + 1)):
            for t in range(3):
                ref[at + 8 * t : at + 8 * t + 8, :] = zero
    for t in range(2):
        w_ref[80 * t + 8 : 80 * t + 8 + ROWS, :] = d_ref[:, t * PATCH : (t + 1) * PATCH]
    w_ref[168 : 168 + ROWS, :] = jnp.where(keep_rows, side_ref[LEVELS * ROWS :, :], 0.0)
    for ref, base, corner in ((above_ref, 0, 72), (below_ref, 8 + ROWS, 32)):
        for t in range(2):
            w_ref[80 * t + base : 80 * t + base + 8, :] = ref[64 + 8 * t : 72 + 8 * t, :]
        w_ref[160 + base : 168 + base, :] = jnp.where(keep, corner_ref[corner : corner + 8, :], 0.0)
    wind = wind_ref[...]
    winds = [wind, wind, jnp.where(keep, wind, 0.0)]
    first_lane, last_lane = lane == 0, lane == PATCH - 1

    for step in range(STEPS):
        src, dst = (a_ref, b_ref) if step % 2 == 0 else (b_ref, a_ref)
        final = step == STEPS - 1
        skip = STEPS if final else 0

        def body(block, carry, src=src, dst=dst, final=final, skip=skip):
            top = pl.multiple_of(24 * (8 * block + skip), 8)

            def tiles(row):
                return [src[pl.ds(top + 24 * row + 8 * t, 8), :] for t in range(3)]

            northern, centre = tiles(0), tiles(1)
            for row in range(8):
                southern = tiles(row + 2)
                right = [pltpu.roll(v, 1, 1) for v in centre]
                left = [pltpu.roll(v, PATCH - 1, 1) for v in centre]
                for t in range(2 if final else 3):
                    west = jnp.where(first_lane, right[(t + 2) % 3], right[t])
                    east = jnp.where(last_lane, left[(t + 1) % 3], left[t])
                    spread = northern[t] + southern[t] + (west + east) - 4.0 * centre[t]
                    d_row = w_ref[pl.ds(80 * t + 8 * block + skip + row + STEPS, 1), :]
                    new = centre[t] + d_row * spread - winds[t] * (centre[t] - west)
                    if final:
                        at = pl.multiple_of(16 * 8 * block, 8) + 16 * row + 8 * t
                        out_ref[pl.ds(at, 8), :] = new
                    else:
                        dst[pl.ds(top + 24 * (row + 1) + 8 * t, 8), :] = new
                northern, centre = centre, southern
            return carry

        lax.fori_loop(0, (TALL - 2 * skip) // 8, body, 0)

    for copy in copies:
        copy.wait()
    for p in range(2):
        live = lane[:1] < count_ref[p]
        precision_out[p : p + 1, :] = jnp.where(live, 1.0 / var_ref[p : p + 1, :], 0.0)


def analysis_kernel(x_ref, obs_ref, precision_ref, site_ref, out_ref, pert_ref):
    members = MEMBERS
    both = 2 * members
    lanes = lax.broadcasted_iota(jnp.int32, (8, PATCH), 1)
    site = site_ref[...]
    level = site // PATCH
    column = site - level * PATCH
    means = [[None] * LEVELS for _ in range(2)]
    perts, weighteds, forcings = [], [], []
    for p in range(2):
        pick = jnp.broadcast_to(column[p : p + 1, :], (members, PATCH))
        got = jnp.zeros((members, PATCH), jnp.float32)
        for l in range(LEVELS):
            block = x_ref[pl.ds(8 * p + l, members, stride=16), :]
            mean = jnp.sum(block, axis=0, keepdims=True) * (1.0 / members)
            means[p][l] = mean
            pert_ref[p * members : (p + 1) * members, l * PATCH : (l + 1) * PATCH] = block - mean
            here = jnp.take_along_axis(block, pick, axis=1, mode="promise_in_bounds")
            got = jnp.where(level[p : p + 1, :] == l, here, got)
        mean = jnp.sum(got, axis=0, keepdims=True) * (1.0 / members)
        pert = got - mean
        weighted = pert * precision_ref[p : p + 1, :]
        perts.append(pert)
        weighteds.append(weighted)
        innovation = obs_ref[p : p + 1, :] - mean
        forcings.append(jnp.sum(weighted * innovation, axis=1, keepdims=True))
    nt = (((1,), (1,)), ((), ()))
    cross = lax.dot_general(
        jnp.concatenate(weighteds, 0), jnp.concatenate(perts, 0), nt,
        precision=HIGHEST, preferred_element_type=jnp.float32,
    )
    row_id = lax.broadcasted_iota(jnp.int32, (both, both), 0)
    col_id = lax.broadcasted_iota(jnp.int32, (both, both), 1)
    eye = (row_id == col_id).astype(jnp.float32)
    system = jnp.where((row_id < members) == (col_id < members), cross, 0.0) + (members - 1.0) * eye
    moved = []

    def spread_steps():
        def mm(a, b):
            return jnp.dot(a, b, precision=HIGHEST, preferred_element_type=jnp.float32)

        squares = jnp.sum(system * system, axis=1, keepdims=True)
        norms = [
            jnp.sqrt(jnp.sum(squares[p * members : (p + 1) * members], axis=0, keepdims=True))
            for p in range(2)
        ]
        norm = jnp.where(row_id[:, :1] < members, norms[0], norms[1])
        iterate = system / norm
        root = update = 1.5 * eye - 0.5 * iterate
        for sweep in range(1, NS_ITERS):
            iterate = mm(iterate, update)
            yield
            update = 1.5 * eye - 0.5 * mm(root, iterate)
            yield
            root = mm(update, root)
            yield
        spread = root * jnp.sqrt((members - 1.0) / norm)
        tn = (((0,), (0,)), ((), ()))
        for l in range(LEVELS):
            moved.append(
                lax.dot_general(
                    spread, pert_ref[:, l * PATCH : (l + 1) * PATCH], tn,
                    precision=HIGHEST, preferred_element_type=jnp.float32,
                )
            )
            yield

    m = system[:members, :] + system[members:, :]
    left = lanes < members
    m = [m[8 * q : 8 * q + 8, :] for q in range(8)]
    f = [
        jnp.where(left, forcings[0][8 * q : 8 * q + 8, :], forcings[1][8 * q : 8 * q + 8, :])
        for q in range(8)
    ]
    sub_id = lax.broadcasted_iota(jnp.int32, (8, PATCH), 0)
    even = sub_id % 2 == 0
    same = [None] * 8
    other = [None] * 8
    steps = spread_steps()
    for k in range(0, members, 2):
        next(steps, None)
        q, r = divmod(k, 8)
        c0, c1 = (
            [jnp.take_along_axis(v, jnp.where(left, j, members + j), axis=1, mode="promise_in_bounds") for v in m]
            for j in (k, k + 1)
        )
        a, b, d = c0[q][r : r + 1, :], c0[q][r + 1 : r + 2, :], c1[q][r + 1 : r + 2, :]
        inv = 1.0 / (a * d - b * b)
        a, b, d = a * inv, b * inv, d * inv
        pair = (sub_id // 2) * 2 == r
        keep_same, keep_other = jnp.where(even, d, a), jnp.broadcast_to(-b, (8, PATCH))
        same[q] = keep_same if r == 0 else jnp.where(pair, keep_same, same[q])
        other[q] = keep_other if r == 0 else jnp.where(pair, keep_other, other[q])
        r0, r1 = m[q][r : r + 1, :], m[q][r + 1 : r + 2, :]
        f0, f1 = f[q][r : r + 1, :], f[q][r + 1 : r + 2, :]
        c0[q], c1[q] = jnp.where(pair, 0.0, c0[q]), jnp.where(pair, 0.0, c1[q])
        r0, r1 = d * r0 - b * r1, a * r1 - b * r0
        f0, f1 = d * f0 - b * f1, a * f1 - b * f0
        m = [v - (u * r0 + w * r1) for v, u, w in zip(m, c0, c1)]
        f = [v - (u * f0 + w * f1) for v, u, w in zip(f, c0, c1)]
    for _ in steps:
        pass
    weight = []
    for q in range(8):
        partner = jnp.where(even, pltpu.roll(f[q], 7, 0), pltpu.roll(f[q], 1, 0))
        weight.append(same[q] * f[q] + other[q] * partner)
    weight = jnp.concatenate(weight, 0)
    turned = pltpu.roll(weight, members, 1)
    left_all = col_id[:members] < members
    for p in range(2):
        wide = jnp.where(left_all, weight, turned) if p == 0 else jnp.where(left_all, turned, weight)
        for l in range(LEVELS):
            rows = slice(p * members, (p + 1) * members)
            shift = jnp.sum(wide * pert_ref[rows, l * PATCH : (l + 1) * PATCH], axis=0, keepdims=True)
            out_ref[pl.ds(8 * p + l, members, stride=16), :] = moved[l][rows] + (means[p][l] + shift)


def unpack_kernel(x_ref, out_ref):
    for l in range(LEVELS):
        for h in range(2):
            out_ref[ROWS * l : ROWS * (l + 1), h * PATCH : (h + 1) * PATCH] = x_ref[
                pl.ds(8 * h + l, ROWS, stride=16), :
            ]


VMEM = pl.BlockSpec(memory_space=pltpu.VMEM)
SMEM = pl.BlockSpec(memory_space=pltpu.SMEM)
HBM = pl.BlockSpec(memory_space=pltpu.HBM)


def f32(*dims):
    return jax.ShapeDtypeStruct(dims, jnp.float32)


def call(kernel, outs, specs, scratch=(), flops=1_000_000, name=None):
    return pl.pallas_call(
        kernel,
        out_shape=outs if len(outs) > 1 else outs[0],
        in_specs=specs,
        out_specs=[VMEM] * len(outs) if len(outs) > 1 else VMEM,
        scratch_shapes=scratch,
        compiler_params=pltpu.CompilerParams(vmem_limit_bytes=VMEM_LIMIT),
        cost_estimate=pl.CostEstimate(flops=flops, bytes_accessed=1_000_000, transcendentals=0),
        name=name,
    )


def on_device(start, diffusivity, stability, observed, variance, site, live):
    rep = lax.axis_index("rep").astype(jnp.int32).reshape(1)
    first, last, side = call(
        pack_kernel,
        [f32(80, PATCH), f32(80, PATCH), f32(LEVELS + 1, ROWS, PATCH)],
        [SMEM, HBM, HBM],
        scratch=[
            pltpu.VMEM((LEVELS, 8, COLS), jnp.float32),
            pltpu.VMEM((LEVELS, 8, COLS), jnp.float32),
            pltpu.VMEM((8, COLS), jnp.float32),
            pltpu.VMEM((8, COLS), jnp.float32),
            pltpu.SemaphoreType.DMA((6,)),
        ],
        name="pack",
    )(rep, start.reshape(LEVELS, ROWS, COLS), diffusivity)
    n = lax.axis_size("sub")
    below = lax.ppermute(first, "sub", [(i + 1, i) for i in range(n - 1)])
    above = lax.ppermute(last, "sub", [(i, i + 1) for i in range(n - 1)])
    swap = [(0, 1), (1, 0)]
    side = lax.ppermute(side, "rep", swap)
    ends = jnp.concatenate([below, above], axis=0).reshape(10, 2, 8, PATCH)
    corner = lax.dynamic_index_in_dim(ends, 1 - rep[0], axis=1, keepdims=False)
    corner = lax.ppermute(corner.reshape(80, PATCH), "rep", swap)
    wind = jnp.broadcast_to(stability.reshape(LEVELS, 1), (LEVELS, PATCH))
    state = pltpu.VMEM((24 * (TALL + 2), PATCH), jnp.float32)
    forecast, obs, precision, cell = call(
        forecast_kernel,
        [f32(ROWS * 16, PATCH), f32(2, PATCH), f32(2, PATCH), jax.ShapeDtypeStruct((2, PATCH), jnp.int32)],
        [SMEM] * 2 + [VMEM] * 7 + [HBM] * 3,
        scratch=[
            state,
            state,
            pltpu.VMEM((3 * (ROWS + 16), PATCH), jnp.float32),
            pltpu.VMEM((2, PATCH), jnp.float32),
            pltpu.SemaphoreType.DMA((3,)),
        ],
        name="forecast",
    )(
        rep,
        live.reshape(2),
        start.reshape(LEVELS * ROWS, COLS),
        diffusivity,
        below,
        above,
        side.reshape((LEVELS + 1) * ROWS, PATCH),
        corner,
        wind,
        observed.reshape(2, PATCH),
        variance.reshape(2, PATCH),
        site.reshape(2, PATCH),
    )
    gathered = lax.all_to_all(forecast.reshape(ROWS, 16, PATCH), GRP, 0, 0, tiled=True)
    analysed = call(
        analysis_kernel,
        [f32(MEMBERS * 16, PATCH)],
        [VMEM] * 4,
        scratch=[pltpu.VMEM((2 * MEMBERS, LEVELS * PATCH), jnp.float32)],
        name="analysis",
    )(gathered.reshape(MEMBERS * 16, PATCH), obs, precision, cell)
    returned = lax.all_to_all(analysed.reshape(MEMBERS, 16, PATCH), GRP, 0, 0, tiled=True)
    out = call(unpack_kernel, [f32(LEVELS * ROWS, COLS)], [VMEM], name="unpack")(
        returned.reshape(ROWS * 16, PATCH)
    )
    return out.reshape(1, LEVELS, ROWS, COLS)


def solution(mesh):
    split = Mesh(
        mesh.devices.reshape(16, 4, mesh.shape["sub"], mesh.shape["rep"]),
        ("grp_0", "grp_1", "sub", "rep"),
    )
    return jax.shard_map(
        on_device,
        mesh=split,
        in_specs=(
            P(GRP, None, "sub", "rep"),
            P("sub", "rep"),
            P(GRP, None),
            P(SUB_GRP, "rep", None),
            P(SUB_GRP, "rep", None),
            P(SUB_GRP, "rep", None),
            P(SUB_GRP, "rep"),
        ),
        out_specs=P(GRP, None, "sub", "rep"),
        check_vma=False,
    )
```

time: 125 us -> 116 us (0.928)
  Pallas kernels: 20.2 us -> 10.9 us
    pallas_call x4, Pallas kernels: 20.2 us -> 10.9 us  [the longest x1 5.18 us: on_device(): call(forecast_kernel, [f32(ROWS * 16, PATCH), f32(2, PATCH), f32(2, PATCH...]
where the time goes in v2:
time: 116 us; the launch traced here: 115 us
  blocking collectives  89.5 us (77%)
  Pallas kernels  10.9 us (9%)
  starting transfers between devices  7.78 us (7%)
  waiting for transfers between devices  3.85 us (3%)
  local copies, waits for them, and re-layouts  3.31 us (3%)
    all_to_all x1, blocking collectives, on_device(): lax.all_to_all(forecast.reshape(ROWS, 16, PATCH), GRP, 0, 0, tiled=True)  51.5 us
    all_to_all x1, blocking collectives, on_device(): lax.all_to_all(analysed.reshape(MEMBERS, 16, PATCH), GRP, 0, 0, tiled=True)  38 us
    pallas_call x1, Pallas kernels, on_device(): call(forecast_kernel, [f32(ROWS * 16, PATCH), f32(2, PATCH), f32(2, PATCH...  5.18 us
    pallas_call x1, Pallas kernels, on_device(): call(analysis_kernel, [f32(MEMBERS * 16, PATCH)], [VMEM] * 4, scratch=[pl...  4.6 us
    unnamed x18, local copies, waits for them, and re-layouts  3.23 us
    ppermute x1, waiting for transfers between devices, on_device(): above = lax.ppermute(last, 'sub', [(i, i + 1) for i in range(n - 1)])  2.66 us
    ppermute x1, starting transfers between devices, on_device(): below = lax.ppermute(first, 'sub', [(i + 1, i) for i in range(n - 1)])  2.65 us
  transfers between devices with their start and end apart: 4, of which 2 were waited for; matrix products, arithmetic and copies ran while one was open for 0% of the time, Pallas kernels for 0%

profile of v2, /device:TPU:24, one launch (start us, length us, event | category | flops | bytes accessed | tf_op | source)
XLA Modules:
  0.0 115.4 jit_solution(7157093933879072716)
XLA Ops:
  0.0 1.0 copy-done
  1.0 0.8 copy-done.2
  1.9 0.2 pack.1
  2.0 2.6 %collective-permute-start = (f32[80,128]{1,0:T(8,128)S(1)}, f32[80,128]{1,0:T(8,128)S(1)}, u32[]{:S(2)}, u32[]{:S(2)}) collective-permute-start(f32[80,128]{1,0:T(8,128)S(1)} %get-tuple-element.12), channel_id=1, source_target_pairs={{2,0},{4,2},{6,4},{3,1},{5,3},{7,5},{10,8},{12,10},{14,12},{11,9},... | collective-permute-start | bytes 122888 | tf_op jit(solution)/shard_map/ppermute | solution.py:304
  4.7 1.3 %collective-permute-start.1 = (f32[80,128]{1,0:T(8,128)S(1)}, f32[80,128]{1,0:T(8,128)S(1)}, u32[]{:S(2)}, u32[]{:S(2)}) collective-permute-start(f32[80,128]{1,0:T(8,128)S(1)} %get-tuple-element.13), channel_id=1, source_target_pairs={{0,2},{2,4},{4,6},{1,3},{3,5},{5,7},{8,10},{10,12},{12,14},{9,11},... | collective-permute-start | bytes 122888 | tf_op jit(solution)/shard_map/ppermute | solution.py:305
  6.0 1.9 %collective-permute-start.2 = (f32[9,64,128]{2,1,0:T(8,128)S(1)}, f32[9,64,128]{2,1,0:T(8,128)S(1)}, u32[]{:S(2)}, u32[]{:S(2)}) collective-permute-start(f32[9,64,128]{2,1,0:T(8,128)S(1)} %get-tuple-element.14), channel_id=1, source_target_pairs={{0,1},{1,0},{2,3},{3,2},{4,5},{5,4},{6,7},{7,6},{8,9},{9,8},{10,11... | collective-permute-start | bytes 884744 | tf_op jit(solution)/shard_map/ppermute | solution.py:307
  7.9 0.0 collective-permute-done.below_ref
  7.9 2.7 %collective-permute-done.1.above_ref = f32[80,128]{1,0:T(8,128)S(1)} collective-permute-done((f32[80,128]{1,0:T(8,128)S(1)}, f32[80,128]{1,0:T(8,128)S(1)}, u32[]{:S(2)}, u32[]{:S(2)}) %collective-permute-start.1) | collective-permute-done | bytes 40992 | tf_op jit(solution)/shard_map/ppermute | solution.py:305
  10.6 1.9 %collective-permute-start.3 = (f32[80,128]{1,0:T(8,128)S(1)}, f32[80,128]{1,0:T(8,128)S(1)}, u32[]{:S(2)}, u32[]{:S(2)}) collective-permute-start(f32[80,128]{1,0:T(8,128)S(1)} %dynamic-slice_bitcast_fusion), channel_id=1, source_target_pairs={{0,1},{1,0},{2,3},{3,2},{4,5},{5,4},{6,7},{7,6},{8,9},{9,8},{10,11... | collective-permute-start | bytes 122888 | tf_op jit(solution)/shard_map/ppermute | solution.py:310
  12.6 1.2 %collective-permute-done.3.corner_ref = f32[80,128]{1,0:T(8,128)S(1)} collective-permute-done((f32[80,128]{1,0:T(8,128)S(1)}, f32[80,128]{1,0:T(8,128)S(1)}, u32[]{:S(2)}, u32[]{:S(2)}) %collective-permute-start.3) | collective-permute-done | bytes 40992 | tf_op jit(solution)/shard_map/ppermute | solution.py:310
  13.7 0.0 collective-permute-done.2
  13.8 0.7 copy-done.8
  14.4 0.1 broadcast_in_dim.8.wind_ref
  14.5 0.0 copy-done.1
  14.5 0.0 copy-done.3
  14.5 0.0 copy-done.5
  14.5 0.0 copy-done.6
  14.5 0.6 copy-done.4
  15.2 0.0 copy-done.7
  15.2 5.2 %forecast.1 = (f32[1024,128]{1,0:T(8,128)S(1)}, f32[2,128]{1,0:T(2,128)S(1)}, f32[2,128]{1,0:T(2,128)S(1)}, s32[2,128]{1,0:T(2,128)S(1)}) custom-call(s32[1]{0:T(128)} %bitcast.rep_ref, s32[2]{0:T(128)S(1)} %bitcast.29, f32[512,256]{1,0:T(8,128)S(1)} %bitcast.22, f32[64,256]{1,0:T(8,128)S(1)} %copy-done.3, f32[80,128]{1,0:T(8,128)S(1)} %collective-permute-done.below_ref, ...), custom_call_target="tpu_custom_call" | custom-call | flops 1000000 | bytes 1000000 | tf_op jit(solution)/shard_map/forecast/pallas_call | solution.py:313
  20.4 51.5 %all_to_all.10 = f32[64,16,128]{2,1,0:T(8,128)S(1)} all-to-all(f32[64,16,128]{2,1,0:T(8,128)S(1)} %bitcast.24), channel_id=1, replica_groups=mesh['grp_0'=16,'grp_1'=4,'sub'=4,'rep'=2] {'grp_0','grp_1'}, dimensions={0} | all-to-all | bytes 1048576 | tf_op jit(solution)/shard_map/all_to_all | solution.py:339
  71.9 4.6 %analysis.1 = f32[1024,128]{1,0:T(8,128)S(1)} custom-call(f32[1024,128]{1,0:T(8,128)S(1)} %bitcast.19, f32[2,128]{1,0:T(2,128)S(1)} %get-tuple-element.16.obs_ref, f32[2,128]{1,0:T(2,128)S(1)} %get-tuple-element.17.precision_ref, s32[2,128]{1,0:T(2,128)S(1)} %get-tuple-element.18.site_ref), custom_call_target="tpu_custom_call" | custom-call | flops 1000000 | bytes 1000000 | tf_op jit(solution)/shard_map/analysis/pallas_call | solution.py:340
  76.5 38.0 %all_to_all.11 = f32[64,16,128]{2,1,0:T(8,128)S(1)} all-to-all(f32[64,16,128]{2,1,0:T(8,128)S(1)} %bitcast.20), channel_id=1, replica_groups=mesh['grp_0'=16,'grp_1'=4,'sub'=4,'rep'=2] {'grp_0','grp_1'}, dimensions={0} | all-to-all | bytes 1048576 | tf_op jit(solution)/shard_map/all_to_all | solution.py:347
  114.5 1.0 unpack.1
  (11 shorter events, 0.0 us)
Async XLA Ops:
  0.0 1.0 copy-start
  1.0 0.8 copy-start.2
  1.9 12.6 %copy-start.1 = (f32[1,8,64,256]{3,2,1,0:T(8,128)S(1)}, f32[1,8,64,256]{3,2,1,0:T(8,128)}, u32[]{:S(2)}) copy-start(f32[1,8,64,256]{3,2,1,0:T(8,128)} %param.7) | copy-start | bytes 1572868
  2.0 5.9 %collective-permute-start = (f32[80,128]{1,0:T(8,128)S(1)}, f32[80,128]{1,0:T(8,128)S(1)}, u32[]{:S(2)}, u32[]{:S(2)}) collective-permute-start(f32[80,128]{1,0:T(8,128)S(1)} %get-tuple-element.12), channel_id=1, source_target_pairs={{2,0},{4,2},{6,4},{3,1},{5,3},{7,5},{10,8},{12,10},{14,12},{11,9},... | collective-permute-start | bytes 122888 | tf_op jit(solution)/shard_map/ppermute | solution.py:304
  4.7 5.9 %collective-permute-start.1 = (f32[80,128]{1,0:T(8,128)S(1)}, f32[80,128]{1,0:T(8,128)S(1)}, u32[]{:S(2)}, u32[]{:S(2)}) collective-permute-start(f32[80,128]{1,0:T(8,128)S(1)} %get-tuple-element.13), channel_id=1, source_target_pairs={{0,2},{2,4},{4,6},{1,3},{3,5},{5,7},{8,10},{10,12},{12,14},{9,11},... | collective-permute-start | bytes 122888 | tf_op jit(solution)/shard_map/ppermute | solution.py:305
  6.0 7.7 %collective-permute-start.2 = (f32[9,64,128]{2,1,0:T(8,128)S(1)}, f32[9,64,128]{2,1,0:T(8,128)S(1)}, u32[]{:S(2)}, u32[]{:S(2)}) collective-permute-start(f32[9,64,128]{2,1,0:T(8,128)S(1)} %get-tuple-element.14), channel_id=1, source_target_pairs={{0,1},{1,0},{2,3},{3,2},{4,5},{5,4},{6,7},{7,6},{8,9},{9,8},{10,11... | collective-permute-start | bytes 884744 | tf_op jit(solution)/shard_map/ppermute | solution.py:307
  10.6 3.9 %copy-start.3 = (f32[64,256]{1,0:T(8,128)S(1)}, f32[64,256]{1,0:T(8,128)}, u32[]{:S(2)}) copy-start(f32[64,256]{1,0:T(8,128)} %d_ref.3) | copy-start | bytes 196612
  10.6 3.1 %collective-permute-start.3 = (f32[80,128]{1,0:T(8,128)S(1)}, f32[80,128]{1,0:T(8,128)S(1)}, u32[]{:S(2)}, u32[]{:S(2)}) collective-permute-start(f32[80,128]{1,0:T(8,128)S(1)} %dynamic-slice_bitcast_fusion), channel_id=1, source_target_pairs={{0,1},{1,0},{2,3},{3,2},{4,5},{5,4},{6,7},{7,6},{8,9},{9,8},{10,11... | collective-permute-start | bytes 122888 | tf_op jit(solution)/shard_map/ppermute | solution.py:310
  13.8 0.8 copy-start.5
  13.8 0.8 copy-start.6
  13.8 0.7 copy-start.8
  14.5 0.7 copy-start.4
  14.5 0.7 copy-start.7

commit v3 on v2

v3 whole, which is shorter than its diff:
```python
import jax
import jax.numpy as jnp
from jax import lax
from jax.experimental import pallas as pl
from jax.experimental.pallas import tpu as pltpu
from jax.sharding import Mesh
from jax.sharding import PartitionSpec as P

LEVELS = 8
PATCH = 128
STEPS = 4
NS_ITERS = 4
MEMBERS = 64
ROWS = 64
COLS = 256
TALL = ROWS + 2 * STEPS
GRP = ("grp_0", "grp_1")
SUB_GRP = ("sub", "grp_0", "grp_1")
HIGHEST = lax.Precision.HIGHEST
VMEM_LIMIT = 24 * 1024 * 1024
PACK_LIMIT = 56 * 1024 * 1024
SUBS = 4
BLOCK = 72


def pack_kernel(
    x_ref, d_ref, stability_ref, obs_hbm, var_hbm, site_hbm, count_hbm, send_ref,
    top_ref, end_ref, dtop_ref, dend_ref, edge_ref, dedge_ref, calm_ref, obs_ref, var_ref, site_ref, count_ref, sems,
):
    y, rep = lax.axis_index("sub"), lax.axis_index("rep")
    half = pl.ds(pl.multiple_of((1 - rep) * PATCH, PATCH), PATCH)
    copies = [
        pltpu.make_async_copy(src, dst, sems.at[i])
        for i, (src, dst) in enumerate(
            (
                (x_ref.at[:, :, half], edge_ref),
                (d_ref.at[:, half], dedge_ref),
                (x_ref.at[:, pl.ds(0, 8), :], top_ref),
                (x_ref.at[:, pl.ds(ROWS - 8, 8), :], end_ref),
                (d_ref.at[pl.ds(0, 8), :], dtop_ref),
                (d_ref.at[pl.ds(ROWS - 8, 8), :], dend_ref),
                (stability_ref, calm_ref),
                (obs_hbm, obs_ref),
                (var_hbm, var_ref),
                (site_hbm, site_ref),
                (count_hbm, count_ref),
            )
        )
    ]
    for copy in copies:
        copy.start()
    sub_id = lax.broadcasted_iota(jnp.int32, (8, PATCH), 0)
    lane = lax.broadcasted_iota(jnp.int32, (8, PATCH), 1)
    for copy in copies:
        copy.wait()
    me = 2 * y + rep
    away = 2 * lax.rem(y + 2, SUBS) + rep
    side_at = pl.multiple_of(BLOCK * (2 * y + 1 - rep), 8)
    for l in range(LEVELS + 1):
        packed = jnp.zeros((8, PATCH), jnp.float32)
        for r in range(8):
            rows = slice(8 * r, 8 * r + 8)
            tile = edge_ref[l, rows, :] if l < LEVELS else dedge_ref[rows, :]
            turned = pltpu.roll(tile, lax.rem(16 * (r + 1 - rep), PATCH), 1)
            packed = jnp.where(lane // 16 == r, turned, packed)
        send_ref[pl.ds(side_at + 8 * l, 8), :] = packed
    for ok, step, rows_ref, d_rows, first in (
        (y > 0, -1, top_ref, dtop_ref, 0),
        (y < SUBS - 1, 1, end_ref, dend_ref, 8 - STEPS),
    ):
        at = pl.multiple_of(BLOCK * jnp.where(ok, me + 2 * step, away), 8)
        corner = pl.multiple_of(BLOCK * jnp.where(ok, 2 * (y + step) + 1 - rep, away), 8)
        for l in range(LEVELS):
            send_ref[pl.ds(corner + l, STEPS, stride=8), :] = edge_ref[
                l, (first // 4) * (ROWS - 8) + first : (first // 4) * (ROWS - 8) + first + STEPS, :
            ]
        send_ref[pl.ds(corner + 32, STEPS), :] = dedge_ref[
            (first // 4) * (ROWS - 8) + first : (first // 4) * (ROWS - 8) + first + STEPS, :
        ]
        for h in range(2):
            cols = slice(h * PATCH, (h + 1) * PATCH)
            for l in range(LEVELS):
                send_ref[pl.ds(at + 8 * h + l, STEPS, stride=16), :] = rows_ref[
                    l, first : first + STEPS, cols
                ]
            send_ref[pl.ds(at + 64 + STEPS * h, STEPS), :] = d_rows[first : first + STEPS, cols]
    own = pl.multiple_of(BLOCK * me, 8)
    picked = jnp.where(sub_id[:, :8] == lane[:, :8], calm_ref[...], 0.0)
    send_ref[pl.ds(own, 8), :] = jnp.broadcast_to(jnp.sum(picked, axis=1, keepdims=True), (LEVELS, PATCH))
    send_ref[pl.ds(own + 8, 2), :] = obs_ref[...]
    for p in range(2):
        live = lane[:1] < count_ref[:, p : p + 1]
        send_ref[pl.ds(own + 10 + p, 1), :] = jnp.where(live, 1.0 / var_ref[p : p + 1, :], 0.0)
    send_ref[pl.ds(own + 12, 2), :] = site_ref[...].astype(jnp.float32)


def forecast_kernel(x_ref, d_ref, got_ref, out_ref, slots_ref, a_ref, b_ref, w_ref):
    y, rep = lax.axis_index("sub"), lax.axis_index("rep")
    lane = lax.broadcasted_iota(jnp.int32, (8, PATCH), 1)
    low = jnp.where(rep == 0, 0, PATCH - STEPS)
    keep = (lane >= low) & (lane < low + STEPS)
    me = 2 * y + rep
    away = 2 * lax.rem(y + 2, SUBS) + rep
    side_at = pl.multiple_of(BLOCK * (2 * y + 1 - rep), 8)
    own = 24 * STEPS
    for l in range(LEVELS + 1):
        packed = got_ref[pl.ds(side_at + 8 * l, 8), :]
        for r in range(8):
            turned = pltpu.roll(packed, lax.rem(PATCH - 16 * (r + rep), PATCH), 1)
            side = jnp.where(keep, turned, 0.0)
            if l < LEVELS:
                a_ref[pl.ds(own + 24 * 8 * r + 16 + l, 8, stride=24), :] = side
            else:
                w_ref[168 + 8 * r : 176 + 8 * r, :] = side
    for l in range(LEVELS):
        for t in range(2):
            a_ref[pl.ds(own + 8 * t + l, ROWS, stride=24), :] = x_ref[
                ROWS * l : ROWS * (l + 1), t * PATCH : (t + 1) * PATCH
            ]
    for t in range(2):
        w_ref[80 * t + 8 : 80 * t + 8 + ROWS, :] = d_ref[:, t * PATCH : (t + 1) * PATCH]
    for ok, step, base, d_base in (
        (y > 0, -1, 0, STEPS),
        (y < SUBS - 1, 1, STEPS + ROWS, 8 + ROWS),
    ):
        at = pl.multiple_of(BLOCK * jnp.where(ok, me + 2 * step, away), 8)
        corner = pl.multiple_of(BLOCK * jnp.where(ok, 2 * (y + step) + 1 - rep, away), 8)
        there = jnp.broadcast_to(ok, (8, PATCH))
        both = keep & there
        for r in range(STEPS):
            to = 24 * (base + r)
            for t in range(2):
                a_ref[to + 8 * t : to + 8 * t + 8, :] = jnp.where(
                    there, got_ref[pl.ds(at + 16 * r + 8 * t, 8), :], 0.0
                )
            a_ref[to + 16 : to + 24, :] = jnp.where(both, got_ref[pl.ds(corner + 8 * r, 8), :], 0.0)
        rows = jnp.where(there, got_ref[pl.ds(at + 64, 8), :], 0.0)
        for t in range(2):
            w_ref[80 * t + d_base : 80 * t + d_base + STEPS, :] = rows[STEPS * t : STEPS * (t + 1)]
        rows = jnp.where(both, got_ref[pl.ds(corner + 32, 8), :], 0.0)
        w_ref[160 + d_base : 160 + d_base + STEPS, :] = rows[:STEPS]
    mine = pl.multiple_of(BLOCK * me, 8)
    wind = got_ref[pl.ds(mine, 8), :]
    slots_ref[...] = got_ref[pl.ds(mine + 8, 8), :]
    winds = [wind, wind, jnp.where(keep, wind, 0.0)]
    first_lane, last_lane = lane == 0, lane == PATCH - 1

    for step in range(STEPS):
        src, dst = (a_ref, b_ref) if step % 2 == 0 else (b_ref, a_ref)
        final = step == STEPS - 1
        skip = STEPS if final else step + 1

        def tiles(row):
            return [src[24 * row + 8 * t : 24 * row + 8 * t + 8, :] for t in range(3)]

        northern, centre = tiles(skip - 1), tiles(skip)
        for row in range(skip, TALL - skip):
            southern = tiles(row + 1)
            right = [pltpu.roll(v, 1, 1) for v in centre]
            left = [pltpu.roll(v, PATCH - 1, 1) for v in centre]
            for t in range(2 if final else 3):
                west = jnp.where(first_lane, right[(t + 2) % 3], right[t])
                east = jnp.where(last_lane, left[(t + 1) % 3], left[t])
                spread = northern[t] + southern[t] + (west + east) - 4.0 * centre[t]
                d_row = w_ref[80 * t + row + STEPS : 80 * t + row + STEPS + 1, :]
                new = centre[t] + d_row * spread - winds[t] * (centre[t] - west)
                if final:
                    at = 16 * (row - skip) + 8 * t
                    out_ref[at : at + 8, :] = new
                else:
                    at = 24 * row + 8 * t
                    dst[at : at + 8, :] = new
            northern, centre = centre, southern


def analysis_kernel(x_ref, slots_ref, out_ref, pert_ref):
    members = MEMBERS
    both = 2 * members
    lanes = lax.broadcasted_iota(jnp.int32, (8, PATCH), 1)
    site = slots_ref[4:6, :].astype(jnp.int32)
    level = site // PATCH
    column = site - level * PATCH
    means = [[None] * LEVELS for _ in range(2)]
    perts, weighteds, forcings = [], [], []
    for p in range(2):
        pick = jnp.broadcast_to(column[p : p + 1, :], (members, PATCH))
        got = jnp.zeros((members, PATCH), jnp.float32)
        for l in range(LEVELS):
            block = x_ref[pl.ds(8 * p + l, members, stride=16), :]
            mean = jnp.sum(block, axis=0, keepdims=True) * (1.0 / members)
            means[p][l] = mean
            pert_ref[p * members : (p + 1) * members, l * PATCH : (l + 1) * PATCH] = block - mean
            here = jnp.take_along_axis(block, pick, axis=1, mode="promise_in_bounds")
            got = jnp.where(level[p : p + 1, :] == l, here, got)
        mean = jnp.sum(got, axis=0, keepdims=True) * (1.0 / members)
        pert = got - mean
        weighted = pert * slots_ref[2 + p : 3 + p, :]
        perts.append(pert)
        weighteds.append(weighted)
        innovation = slots_ref[p : p + 1, :] - mean
        forcings.append(jnp.sum(weighted * innovation, axis=1, keepdims=True))
    nt = (((1,), (1,)), ((), ()))
    cross = lax.dot_general(
        jnp.concatenate(weighteds, 0), jnp.concatenate(perts, 0), nt,
        precision=HIGHEST, preferred_element_type=jnp.float32,
    )
    row_id = lax.broadcasted_iota(jnp.int32, (both, both), 0)
    col_id = lax.broadcasted_iota(jnp.int32, (both, both), 1)
    eye = (row_id == col_id).astype(jnp.float32)
    system = jnp.where((row_id < members) == (col_id < members), cross, 0.0) + (members - 1.0) * eye
    moved = []

    def spread_steps():
        def mm(a, b):
            return jnp.dot(a, b, precision=HIGHEST, preferred_element_type=jnp.float32)

        squares = jnp.sum(system * system, axis=1, keepdims=True)
        norms = [
            jnp.sqrt(jnp.sum(squares[p * members : (p + 1) * members], axis=0, keepdims=True))
            for p in range(2)
        ]
        norm = jnp.where(row_id[:, :1] < members, norms[0], norms[1])
        iterate = system / norm
        root = update = 1.5 * eye - 0.5 * iterate
        for sweep in range(1, NS_ITERS):
            iterate = mm(iterate, update)
            yield
            update = 1.5 * eye - 0.5 * mm(root, iterate)
            yield
            root = mm(update, root)
            yield
        spread = root * jnp.sqrt((members - 1.0) / norm)
        tn = (((0,), (0,)), ((), ()))
        for l in range(LEVELS):
            moved.append(
                lax.dot_general(
                    spread, pert_ref[:, l * PATCH : (l + 1) * PATCH], tn,
                    precision=HIGHEST, preferred_element_type=jnp.float32,
                )
            )
            yield

    m = system[:members, :] + system[members:, :]
    left = lanes < members
    m = [m[8 * q : 8 * q + 8, :] for q in range(8)]
    f = [
        jnp.where(left, forcings[0][8 * q : 8 * q + 8, :], forcings[1][8 * q : 8 * q + 8, :])
        for q in range(8)
    ]
    sub_id = lax.broadcasted_iota(jnp.int32, (8, PATCH), 0)
    even = sub_id % 2 == 0
    same = [None] * 8
    other = [None] * 8
    steps = spread_steps()
    for k in range(0, members, 2):
        next(steps, None)
        q, r = divmod(k, 8)
        c0, c1 = (
            [jnp.take_along_axis(v, jnp.where(left, j, members + j), axis=1, mode="promise_in_bounds") for v in m]
            for j in (k, k + 1)
        )
        a, b, d = c0[q][r : r + 1, :], c0[q][r + 1 : r + 2, :], c1[q][r + 1 : r + 2, :]
        inv = 1.0 / (a * d - b * b)
        a, b, d = a * inv, b * inv, d * inv
        pair = (sub_id // 2) * 2 == r
        keep_same, keep_other = jnp.where(even, d, a), jnp.broadcast_to(-b, (8, PATCH))
        same[q] = keep_same if r == 0 else jnp.where(pair, keep_same, same[q])
        other[q] = keep_other if r == 0 else jnp.where(pair, keep_other, other[q])
        r0, r1 = m[q][r : r + 1, :], m[q][r + 1 : r + 2, :]
        f0, f1 = f[q][r : r + 1, :], f[q][r + 1 : r + 2, :]
        c0[q], c1[q] = jnp.where(pair, 0.0, c0[q]), jnp.where(pair, 0.0, c1[q])
        r0, r1 = d * r0 - b * r1, a * r1 - b * r0
        f0, f1 = d * f0 - b * f1, a * f1 - b * f0
        m = [v - (u * r0 + w * r1) for v, u, w in zip(m, c0, c1)]
        f = [v - (u * f0 + w * f1) for v, u, w in zip(f, c0, c1)]
    for _ in steps:
        pass
    weight = []
    for q in range(8):
        partner = jnp.where(even, pltpu.roll(f[q], 7, 0), pltpu.roll(f[q], 1, 0))
        weight.append(same[q] * f[q] + other[q] * partner)
    weight = jnp.concatenate(weight, 0)
    turned = pltpu.roll(weight, members, 1)
    left_all = col_id[:members] < members
    for p in range(2):
        wide = jnp.where(left_all, weight, turned) if p == 0 else jnp.where(left_all, turned, weight)
        for l in range(LEVELS):
            rows = slice(p * members, (p + 1) * members)
            shift = jnp.sum(wide * pert_ref[rows, l * PATCH : (l + 1) * PATCH], axis=0, keepdims=True)
            out_ref[pl.ds(8 * p + l, members, stride=16), :] = moved[l][rows] + (means[p][l] + shift)


def unpack_kernel(x_ref, out_ref):
    for l in range(LEVELS):
        for h in range(2):
            out_ref[ROWS * l : ROWS * (l + 1), h * PATCH : (h + 1) * PATCH] = x_ref[
                pl.ds(8 * h + l, ROWS, stride=16), :
            ]


VMEM = pl.BlockSpec(memory_space=pltpu.VMEM)
SMEM = pl.BlockSpec(memory_space=pltpu.SMEM)
HBM = pl.BlockSpec(memory_space=pltpu.HBM)


def f32(*dims):
    return jax.ShapeDtypeStruct(dims, jnp.float32)


def call(kernel, outs, specs, scratch=(), flops=1_000_000, name=None, limit=VMEM_LIMIT):
    return pl.pallas_call(
        kernel,
        out_shape=outs if len(outs) > 1 else outs[0],
        in_specs=specs,
        out_specs=[VMEM] * len(outs) if len(outs) > 1 else VMEM,
        scratch_shapes=scratch,
        compiler_params=pltpu.CompilerParams(vmem_limit_bytes=limit),
        cost_estimate=pl.CostEstimate(flops=flops, bytes_accessed=1_000_000, transcendentals=0),
        name=name,
    )


def on_device(start, diffusivity, stability, observed, variance, site, live):
    def vmem(*dims, dtype=jnp.float32):
        return pltpu.VMEM(dims, dtype)

    send = call(
        pack_kernel,
        [f32(2 * SUBS * BLOCK, PATCH)],
        [HBM] * 7,
        scratch=[
            vmem(LEVELS, 8, COLS),
            vmem(LEVELS, 8, COLS),
            vmem(8, COLS),
            vmem(8, COLS),
            vmem(LEVELS, ROWS, PATCH),
            vmem(ROWS, PATCH),
            vmem(1, LEVELS),
            vmem(2, PATCH),
            vmem(2, PATCH),
            vmem(2, PATCH, dtype=jnp.int32),
            vmem(1, 2, dtype=jnp.int32),
            pltpu.SemaphoreType.DMA((11,)),
        ],
        name="pack",
        limit=PACK_LIMIT,
    )(
        start.reshape(LEVELS, ROWS, COLS),
        diffusivity,
        stability,
        observed.reshape(2, PATCH),
        variance.reshape(2, PATCH),
        site.reshape(2, PATCH),
        live,
    )
    got = lax.all_to_all(send.reshape(2 * SUBS, BLOCK, PATCH), ("sub", "rep"), 0, 0, tiled=True)
    forecast, slots = call(
        forecast_kernel,
        [f32(ROWS * 16, PATCH), f32(8, PATCH)],
        [VMEM] * 3,
        scratch=[vmem(24 * TALL, PATCH), vmem(24 * TALL, PATCH), vmem(3 * (ROWS + 16), PATCH)],
        name="forecast",
    )(start.reshape(LEVELS * ROWS, COLS), diffusivity, got.reshape(2 * SUBS * BLOCK, PATCH))
    gathered = lax.all_to_all(forecast.reshape(ROWS, 16, PATCH), GRP, 0, 0, tiled=True)
    analysed = call(
        analysis_kernel,
        [f32(MEMBERS * 16, PATCH)],
        [VMEM] * 2,
        scratch=[pltpu.VMEM((2 * MEMBERS, LEVELS * PATCH), jnp.float32)],
        name="analysis",
    )(gathered.reshape(MEMBERS * 16, PATCH), slots)
    returned = lax.all_to_all(analysed.reshape(MEMBERS, 16, PATCH), GRP, 0, 0, tiled=True)
    out = call(unpack_kernel, [f32(LEVELS * ROWS, COLS)], [VMEM], name="unpack")(
        returned.reshape(ROWS * 16, PATCH)
    )
    return out.reshape(1, LEVELS, ROWS, COLS)


def solution(mesh):
    split = Mesh(
        mesh.devices.reshape(16, 4, mesh.shape["sub"], mesh.shape["rep"]),
        ("grp_0", "grp_1", "sub", "rep"),
    )
    return jax.shard_map(
        on_device,
        mesh=split,
        in_specs=(
            P(GRP, None, "sub", "rep"),
            P("sub", "rep"),
            P(GRP, None),
            P(SUB_GRP, "rep", None),
            P(SUB_GRP, "rep", None),
            P(SUB_GRP, "rep", None),
            P(SUB_GRP, "rep"),
        ),
        out_specs=P(GRP, None, "sub", "rep"),
        check_vma=False,
    )
```

time: 116 us -> 111 us (0.957)
  blocking collectives: 89.5 us -> 99.6 us
  starting transfers between devices: 7.78 us -> 0 us
  waiting for transfers between devices: 3.85 us -> 0 us
  local copies, waits for them, and re-layouts: 3.31 us -> 0.01 us
  Pallas kernels: 10.9 us -> 9.63 us
    all_to_all x0 -> x1, blocking collectives: none -> 14.9 us  [on_device(): lax.all_to_all(send.reshape(2 * SUBS, BLOCK, PATCH), ('sub', 'rep'), 0, 0...]
    ppermute x4 -> x0, starting transfers between devices: 7.78 us -> none  [the longest x1 2.65 us: on_device(): below = lax.ppermute(first, 'sub', [(i + 1, i) for i in range(n - 1)])]
    all_to_all x1, blocking collectives: 51.5 us -> 47.1 us  [on_device(): lax.all_to_all(forecast.reshape(ROWS, 16, PATCH), GRP, 0, 0, tiled=True)]
    ppermute x4 -> x0, waiting for transfers between devices: 3.85 us -> none  [the longest x1 2.66 us: on_device(): above = lax.ppermute(last, 'sub', [(i, i + 1) for i in range(n - 1)])]
    unnamed x18 -> x4, local copies, waits for them, and re-layouts: 3.23 us -> 0.01 us
    pallas_call x3, Pallas kernels: 9.93 us -> 8.68 us  [the longest x1 4.6 us: on_device(): call(analysis_kernel, [f32(MEMBERS * 16, PATCH)], [VMEM] * 2, scratch=[pl...]
  transfers between devices with their start and end apart: 4 -> 0, of which waited for: 2 -> 0; matrix products, arithmetic and copies ran while one was open for 0% -> 0% of each run, Pallas kernels for 0% -> 0%
where the time goes in v3:
time: 111 us; the launch traced here: 109 us
  blocking collectives  99.6 us (90%)
  Pallas kernels  9.63 us (9%)
    all_to_all x1, blocking collectives, on_device(): lax.all_to_all(forecast.reshape(ROWS, 16, PATCH), GRP, 0, 0, tiled=True)  47.1 us
    all_to_all x1, blocking collectives, on_device(): lax.all_to_all(analysed.reshape(MEMBERS, 16, PATCH), GRP, 0, 0, tiled=True)  37.7 us
    all_to_all x1, blocking collectives, on_device(): lax.all_to_all(send.reshape(2 * SUBS, BLOCK, PATCH), ('sub', 'rep'), 0, 0...  14.9 us
    pallas_call x1, Pallas kernels, on_device(): call(analysis_kernel, [f32(MEMBERS * 16, PATCH)], [VMEM] * 2, scratch=[pl...  4.6 us

profile of v3, /device:TPU:24, one launch (start us, length us, event | category | flops | bytes accessed | tf_op | source)
XLA Modules:
  0.0 109.3 jit_solution(1275032838104938818)
XLA Ops:
  0.0 0.0 copy-start
  0.0 2.0 %pack.1 = f32[576,128]{1,0:T(8,128)} custom-call(f32[8,64,256]{2,1,0:T(8,128)} %bitcast.12, f32[64,256]{1,0:T(8,128)} %d_ref.3, f32[1,8]{1,0:T(1,128)} %stability_ref.1, f32[2,128]{1,0:T(2,128)} %bitcast.20, f32[2,128]{1,0:T(2,128)} %bitcast.21, s32[2,128]{1,0:T(2,128)} %bitcast.22, s32[1,2]{1,0:T(1,128)} %count_hbm.1), custom_call_target="tpu_custom_call" | custom-call | flops 1000000 | bytes 1000000 | tf_op jit(solution)/shard_map/pack/pallas_call | solution.py:327
  2.0 0.0 copy-start.1
  2.0 14.9 %all_to_all.15 = f32[8,72,128]{2,1,0:T(8,128)S(1)} all-to-all(f32[8,72,128]{2,1,0:T(8,128)} %bitcast.19), channel_id=1, replica_groups=mesh['grp_0'=16,'grp_1'=4,'sub'=4,'rep'=2] {'sub','rep'}, dimensions={0} | all-to-all | bytes 589824 | tf_op jit(solution)/shard_map/all_to_all | solution.py:356
  16.9 0.0 copy-done
  16.9 0.0 copy-done.1
  16.9 2.1 %forecast.1 = (f32[1024,128]{1,0:T(8,128)S(1)}, f32[8,128]{1,0:T(8,128)S(1)}) custom-call(f32[512,256]{1,0:T(8,128)S(1)} %bitcast.13, f32[64,256]{1,0:T(8,128)S(1)} %copy-done.1, f32[576,128]{1,0:T(8,128)S(1)} %bitcast.17), custom_call_target="tpu_custom_call" | custom-call | flops 1000000 | bytes 1000000 | tf_op jit(solution)/shard_map/forecast/pallas_call | solution.py:357
  19.0 47.1 %all_to_all.16 = f32[64,16,128]{2,1,0:T(8,128)S(1)} all-to-all(f32[64,16,128]{2,1,0:T(8,128)S(1)} %bitcast.18), channel_id=1, replica_groups=mesh['grp_0'=16,'grp_1'=4,'sub'=4,'rep'=2] {'grp_0','grp_1'}, dimensions={0} | all-to-all | bytes 1048576 | tf_op jit(solution)/shard_map/all_to_all | solution.py:364
  66.1 4.6 %analysis.1 = f32[1024,128]{1,0:T(8,128)S(1)} custom-call(f32[1024,128]{1,0:T(8,128)S(1)} %bitcast.14, f32[8,128]{1,0:T(8,128)S(1)} %get-tuple-element.8.slots_ref), custom_call_target="tpu_custom_call" | custom-call | flops 1000000 | bytes 1000000 | tf_op jit(solution)/shard_map/analysis/pallas_call | solution.py:365
  70.7 37.7 %all_to_all.17 = f32[64,16,128]{2,1,0:T(8,128)S(1)} all-to-all(f32[64,16,128]{2,1,0:T(8,128)S(1)} %bitcast.15), channel_id=1, replica_groups=mesh['grp_0'=16,'grp_1'=4,'sub'=4,'rep'=2] {'grp_0','grp_1'}, dimensions={0} | all-to-all | bytes 1048576 | tf_op jit(solution)/shard_map/all_to_all | solution.py:372
  108.3 1.0 unpack.1
Async XLA Ops:
  0.0 16.9 %copy-start = (f32[1,8,64,256]{3,2,1,0:T(8,128)S(1)}, f32[1,8,64,256]{3,2,1,0:T(8,128)}, u32[]{:S(2)}) copy-start(f32[1,8,64,256]{3,2,1,0:T(8,128)} %param.7) | copy-start | bytes 1572868
  2.0 14.9 %copy-start.1 = (f32[64,256]{1,0:T(8,128)S(1)}, f32[64,256]{1,0:T(8,128)}, u32[]{:S(2)}) copy-start(f32[64,256]{1,0:T(8,128)} %d_ref.3) | copy-start | bytes 196612

commit v4 on v3

--- a/solution.py
+++ b/solution.py
@@ -18,7 +18,6 @@
 SUB_GRP = ("sub", "grp_0", "grp_1")
 HIGHEST = lax.Precision.HIGHEST
 VMEM_LIMIT = 24 * 1024 * 1024
-PACK_LIMIT = 56 * 1024 * 1024
 SUBS = 4
 BLOCK = 72
 
@@ -176,22 +175,21 @@
 def analysis_kernel(x_ref, slots_ref, out_ref, pert_ref):
     members = MEMBERS
     both = 2 * members
-    lanes = lax.broadcasted_iota(jnp.int32, (8, PATCH), 1)
+    tile = (8, PATCH)
+    lanes = lax.broadcasted_iota(jnp.int32, tile, 1)
+    sub_id = lax.broadcasted_iota(jnp.int32, tile, 0)
+    left = lanes < members
     site = slots_ref[4:6, :].astype(jnp.int32)
     level = site // PATCH
     column = site - level * PATCH
-    means = [[None] * LEVELS for _ in range(2)]
     perts, weighteds, forcings = [], [], []
     for p in range(2):
         pick = jnp.broadcast_to(column[p : p + 1, :], (members, PATCH))
-        got = jnp.zeros((members, PATCH), jnp.float32)
+        got = None
         for l in range(LEVELS):
             block = x_ref[pl.ds(8 * p + l, members, stride=16), :]
-            mean = jnp.sum(block, axis=0, keepdims=True) * (1.0 / members)
-            means[p][l] = mean
-            pert_ref[p * members : (p + 1) * members, l * PATCH : (l + 1) * PATCH] = block - mean
             here = jnp.take_along_axis(block, pick, axis=1, mode="promise_in_bounds")
-            got = jnp.where(level[p : p + 1, :] == l, here, got)
+            got = here if got is None else jnp.where(level[p : p + 1, :] == l, here, got)
         mean = jnp.sum(got, axis=0, keepdims=True) * (1.0 / members)
         pert = got - mean
         weighted = pert * slots_ref[2 + p : 3 + p, :]
@@ -200,34 +198,57 @@
         innovation = slots_ref[p : p + 1, :] - mean
         forcings.append(jnp.sum(weighted * innovation, axis=1, keepdims=True))
     nt = (((1,), (1,)), ((), ()))
+    zero = jnp.zeros((members, PATCH), jnp.float32)
+    pair = jnp.concatenate(
+        [jnp.concatenate([perts[0], zero], 1), jnp.concatenate([zero, perts[1]], 1)], 0
+    )
     cross = lax.dot_general(
-        jnp.concatenate(weighteds, 0), jnp.concatenate(perts, 0), nt,
+        jnp.concatenate(weighteds, 1), pair, nt,
         precision=HIGHEST, preferred_element_type=jnp.float32,
     )
-    row_id = lax.broadcasted_iota(jnp.int32, (both, both), 0)
-    col_id = lax.broadcasted_iota(jnp.int32, (both, both), 1)
-    eye = (row_id == col_id).astype(jnp.float32)
-    system = jnp.where((row_id < members) == (col_id < members), cross, 0.0) + (members - 1.0) * eye
+    row_id = lax.broadcasted_iota(jnp.int32, (members, PATCH), 0)
+    col_id = lax.broadcasted_iota(jnp.int32, (members, PATCH), 1)
+    left_all = col_id < members
+    on_diagonal = row_id == col_id - jnp.where(left_all, 0, members)
+    m = cross + jnp.where(on_diagonal, members - 1.0, 0.0)
+    system = jnp.concatenate([jnp.where(left_all, m, 0.0), jnp.where(left_all, 0.0, m)], 0)
+    means = [[None] * LEVELS for _ in range(2)]
     moved = []
 
     def spread_steps():
         def mm(a, b):
             return jnp.dot(a, b, precision=HIGHEST, preferred_element_type=jnp.float32)
+
+        def centre(l):
+            for p in range(2):
+                block = x_ref[pl.ds(8 * p + l, members, stride=16), :]
+                mean = jnp.sum(block, axis=0, keepdims=True) * (1.0 / members)
+                means[p][l] = mean
+                pert_ref[p * members : (p + 1) * members, l * PATCH : (l + 1) * PATCH] = block - mean
 
         squares = jnp.sum(system * system, axis=1, keepdims=True)
         norms = [
             jnp.sqrt(jnp.sum(squares[p * members : (p + 1) * members], axis=0, keepdims=True))
             for p in range(2)
         ]
-        norm = jnp.where(row_id[:, :1] < members, norms[0], norms[1])
+        first_half = lax.broadcasted_iota(jnp.int32, (both, 1), 0) < members
+        norm = jnp.where(first_half, norms[0], norms[1])
+        eye = (
+            lax.broadcasted_iota(jnp.int32, (both, both), 0)
+            == lax.broadcasted_iota(jnp.int32, (both, both), 1)
+        ).astype(jnp.float32)
         iterate = system / norm
         root = update = 1.5 * eye - 0.5 * iterate
         for sweep in range(1, NS_ITERS):
             iterate = mm(iterate, update)
+            centre(3 * sweep - 3)
             yield
             update = 1.5 * eye - 0.5 * mm(root, iterate)
+            centre(3 * sweep - 2)
             yield
             root = mm(update, root)
+            if 3 * sweep - 1 < LEVELS:
+                centre(3 * sweep - 1)
             yield
         spread = root * jnp.sqrt((members - 1.0) / norm)
         tn = (((0,), (0,)), ((), ()))
@@ -240,48 +261,74 @@
             )
             yield
 
-    m = system[:members, :] + system[members:, :]
-    left = lanes < members
     m = [m[8 * q : 8 * q + 8, :] for q in range(8)]
     f = [
         jnp.where(left, forcings[0][8 * q : 8 * q + 8, :], forcings[1][8 * q : 8 * q + 8, :])
         for q in range(8)
     ]
-    sub_id = lax.broadcasted_iota(jnp.int32, (8, PATCH), 0)
-    even = sub_id % 2 == 0
-    same = [None] * 8
-    other = [None] * 8
+    inverse = [[None] * 4 for _ in range(8)]
     steps = spread_steps()
-    for k in range(0, members, 2):
+
+    def spread_row(v, row):
+        return jnp.broadcast_to(v[row : row + 1, :], tile)
+
+    for k in range(0, members, 4):
         next(steps, None)
         q, r = divmod(k, 8)
-        c0, c1 = (
+        c = [
             [jnp.take_along_axis(v, jnp.where(left, j, members + j), axis=1, mode="promise_in_bounds") for v in m]
-            for j in (k, k + 1)
-        )
-        a, b, d = c0[q][r : r + 1, :], c0[q][r + 1 : r + 2, :], c1[q][r + 1 : r + 2, :]
-        inv = 1.0 / (a * d - b * b)
-        a, b, d = a * inv, b * inv, d * inv
-        pair = (sub_id // 2) * 2 == r
-        keep_same, keep_other = jnp.where(even, d, a), jnp.broadcast_to(-b, (8, PATCH))
-        same[q] = keep_same if r == 0 else jnp.where(pair, keep_same, same[q])
-        other[q] = keep_other if r == 0 else jnp.where(pair, keep_other, other[q])
-        r0, r1 = m[q][r : r + 1, :], m[q][r + 1 : r + 2, :]
-        f0, f1 = f[q][r : r + 1, :], f[q][r + 1 : r + 2, :]
-        c0[q], c1[q] = jnp.where(pair, 0.0, c0[q]), jnp.where(pair, 0.0, c1[q])
-        r0, r1 = d * r0 - b * r1, a * r1 - b * r0
-        f0, f1 = d * f0 - b * f1, a * f1 - b * f0
-        m = [v - (u * r0 + w * r1) for v, u, w in zip(m, c0, c1)]
-        f = [v - (u * f0 + w * f1) for v, u, w in zip(f, c0, c1)]
+            for j in range(k, k + 4)
+        ]
+        b = [[spread_row(c[j][q], r + i) for j in range(4)] for i in range(4)]
+        det = 1.0 / (b[0][0] * b[1][1] - b[0][1] * b[0][1])
+        a00, a01, a11 = b[1][1] * det, -b[0][1] * det, b[0][0] * det
+        e00, e01 = a00 * b[0][2] + a01 * b[1][2], a00 * b[0][3] + a01 * b[1][3]
+        e10, e11 = a01 * b[0][2] + a11 * b[1][2], a01 * b[0][3] + a11 * b[1][3]
+        s00 = b[2][2] - (b[0][2] * e00 + b[1][2] * e10)
+        s01 = b[2][3] - (b[0][2] * e01 + b[1][2] * e11)
+        s11 = b[3][3] - (b[0][3] * e01 + b[1][3] * e11)
+        det = 1.0 / (s00 * s11 - s01 * s01)
+        t00, t01, t11 = s11 * det, -s01 * det, s00 * det
+        g00, g01 = e00 * t00 + e01 * t01, e00 * t01 + e01 * t11
+        g10, g11 = e10 * t00 + e11 * t01, e10 * t01 + e11 * t11
+        x01 = a01 + (g00 * e10 + g01 * e11)
+        x = [
+            [a00 + (g00 * e00 + g01 * e01), x01, -g00, -g01],
+            [x01, a11 + (g10 * e10 + g11 * e11), -g10, -g11],
+            [-g00, -g10, t00, t01],
+            [-g01, -g11, t01, t11],
+        ]
+        rows = [spread_row(m[q], r + i) for i in range(4)]
+        loads = [spread_row(f[q], r + i) for i in range(4)]
+        for j in range(4):
+            for i in range(4):
+                old = inverse[q][j]
+                inverse[q][j] = x[i][j] if old is None else jnp.where(sub_id == r + i, x[i][j], old)
+        rows = [(x[i][0] * rows[0] + x[i][1] * rows[1]) + (x[i][2] * rows[2] + x[i][3] * rows[3]) for i in range(4)]
+        loads = [(x[i][0] * loads[0] + x[i][1] * loads[1]) + (x[i][2] * loads[2] + x[i][3] * loads[3]) for i in range(4)]
+        pivot = (sub_id >= r) & (sub_id < r + 4)
+        for i in range(4):
+            c[i][q] = jnp.where(pivot, 0.0, c[i][q])
+        if k < members - 4:
+            m = [
+                m[n] - ((c[0][n] * rows[0] + c[1][n] * rows[1]) + (c[2][n] * rows[2] + c[3][n] * rows[3]))
+                for n in range(8)
+            ]
+        f = [
+            f[n] - ((c[0][n] * loads[0] + c[1][n] * loads[1]) + (c[2][n] * loads[2] + c[3][n] * loads[3]))
+            for n in range(8)
+        ]
     for _ in steps:
         pass
     weight = []
     for q in range(8):
-        partner = jnp.where(even, pltpu.roll(f[q], 7, 0), pltpu.roll(f[q], 1, 0))
-        weight.append(same[q] * f[q] + other[q] * partner)
+        terms = [
+            inverse[q][j] * jnp.where(sub_id < 4, f[q][j : j + 1, :], f[q][4 + j : 5 + j, :])
+            for j in range(4)
+        ]
+        weight.append((terms[0] + terms[1]) + (terms[2] + terms[3]))
     weight = jnp.concatenate(weight, 0)
     turned = pltpu.roll(weight, members, 1)
-    left_all = col_id[:members] < members
     for p in range(2):
         wide = jnp.where(left_all, weight, turned) if p == 0 else jnp.where(left_all, turned, weight)
         for l in range(LEVELS):
@@ -290,12 +337,18 @@
             out_ref[pl.ds(8 * p + l, members, stride=16), :] = moved[l][rows] + (means[p][l] + shift)
 
 
-def unpack_kernel(x_ref, out_ref):
+def unpack_kernel(x_ref, out_hbm, out_ref, sems):
+    copies = []
     for l in range(LEVELS):
+        rows = slice(ROWS * l, ROWS * (l + 1))
         for h in range(2):
-            out_ref[ROWS * l : ROWS * (l + 1), h * PATCH : (h + 1) * PATCH] = x_ref[
-                pl.ds(8 * h + l, ROWS, stride=16), :
-            ]
+            out_ref[rows, h * PATCH : (h + 1) * PATCH] = x_ref[pl.ds(8 * h + l, ROWS, stride=16), :]
+        if l % 2:
+            some = pl.ds(ROWS * (l - 1), 2 * ROWS)
+            copies.append(pltpu.make_async_copy(out_ref.at[some], out_hbm.at[some], sems.at[l // 2]))
+            copies[-1].start()
+    for copy in copies:
+        copy.wait()
 
 
 VMEM = pl.BlockSpec(memory_space=pltpu.VMEM)
@@ -307,14 +360,14 @@
     return jax.ShapeDtypeStruct(dims, jnp.float32)
 
 
-def call(kernel, outs, specs, scratch=(), flops=1_000_000, name=None, limit=VMEM_LIMIT):
+def call(kernel, outs, specs, scratch=(), flops=1_000_000, name=None, to=VMEM):
     return pl.pallas_call(
         kernel,
         out_shape=outs if len(outs) > 1 else outs[0],
         in_specs=specs,
-        out_specs=[VMEM] * len(outs) if len(outs) > 1 else VMEM,
+        out_specs=[to] * len(outs) if len(outs) > 1 else to,
         scratch_shapes=scratch,
-        compiler_params=pltpu.CompilerParams(vmem_limit_bytes=limit),
+        compiler_params=pltpu.CompilerParams(vmem_limit_bytes=VMEM_LIMIT),
         cost_estimate=pl.CostEstimate(flops=flops, bytes_accessed=1_000_000, transcendentals=0),
         name=name,
     )
@@ -343,15 +396,19 @@
             pltpu.SemaphoreType.DMA((11,)),
         ],
         name="pack",
-        limit=PACK_LIMIT,
     )(
-        start.reshape(LEVELS, ROWS, COLS),
-        diffusivity,
-        stability,
-        observed.reshape(2, PATCH),
-        variance.reshape(2, PATCH),
-        site.reshape(2, PATCH),
-        live,
+        *(
+            pltpu.with_memory_space_constraint(v, pltpu.HBM)
+            for v in (
+                start.reshape(LEVELS, ROWS, COLS),
+                diffusivity,
+                stability,
+                observed.reshape(2, PATCH),
+                variance.reshape(2, PATCH),
+                site.reshape(2, PATCH),
+                live,
+            )
+        )
     )
     got = lax.all_to_all(send.reshape(2 * SUBS, BLOCK, PATCH), ("sub", "rep"), 0, 0, tiled=True)
     forecast, slots = call(
@@ -370,7 +427,14 @@
         name="analysis",
     )(gathered.reshape(MEMBERS * 16, PATCH), slots)
     returned = lax.all_to_all(analysed.reshape(MEMBERS, 16, PATCH), GRP, 0, 0, tiled=True)
-    out = call(unpack_kernel, [f32(LEVELS * ROWS, COLS)], [VMEM], name="unpack")(
+    out = call(
+        unpack_kernel,
+        [f32(LEVELS * ROWS, COLS)],
+        [VMEM],
+        scratch=[vmem(LEVELS * ROWS, COLS), pltpu.SemaphoreType.DMA((LEVELS // 2,))],
+        name="unpack",
+        to=HBM,
+    )(
         returned.reshape(ROWS * 16, PATCH)
     )
     return out.reshape(1, LEVELS, ROWS, COLS)

time: 111 us -> 110 us (level)
  Pallas kernels: 9.63 us -> 8.09 us
where the time goes in v4:
time: 110 us; the launch traced here: 108 us
  blocking collectives  99.4 us (90%)
  Pallas kernels  8.09 us (7%)
    all_to_all x1, blocking collectives, on_device(): lax.all_to_all(forecast.reshape(ROWS, 16, PATCH), GRP, 0, 0, tiled=True)  47.8 us
    all_to_all x1, blocking collectives, on_device(): lax.all_to_all(analysed.reshape(MEMBERS, 16, PATCH), GRP, 0, 0, tiled=True)  37.7 us
    all_to_all x1, blocking collectives, on_device(): lax.all_to_all(send.reshape(2 * SUBS, BLOCK, PATCH), ('sub', 'rep'), 0, 0...  13.9 us
    pallas_call x1, Pallas kernels, on_device(): call(analysis_kernel, [f32(MEMBERS * 16, PATCH)], [VMEM] * 2, scratch=[pl...  3.85 us

profile of v4, /device:TPU:24, one launch (start us, length us, event | category | flops | bytes accessed | tf_op | source)
XLA Modules:
  0.0 107.5 jit_solution(17414546202913216152)
XLA Ops:
  0.0 0.0 copy-start
  0.0 1.3 %pack.1 = f32[576,128]{1,0:T(8,128)S(1)} custom-call(f32[8,64,256]{2,1,0:T(8,128)} %bitcast.12, f32[64,256]{1,0:T(8,128)} %d_ref.3, f32[1,8]{1,0:T(1,128)} %stability_ref.1, f32[2,128]{1,0:T(2,128)} %bitcast.20, f32[2,128]{1,0:T(2,128)} %bitcast.21, s32[2,128]{1,0:T(2,128)} %bitcast.22, s32[1,2]{1,0:T(1,128)} %count_hbm.1), custom_call_target="tpu_custom_call" | custom-call | flops 1000000 | bytes 1000000 | tf_op jit(solution)/shard_map/pack/pallas_call | solution.py:380
  1.3 0.0 copy-start.1
  1.3 13.9 %all_to_all.15 = f32[8,72,128]{2,1,0:T(8,128)S(1)} all-to-all(f32[8,72,128]{2,1,0:T(8,128)S(1)} %bitcast.18), channel_id=1, replica_groups=mesh['grp_0'=16,'grp_1'=4,'sub'=4,'rep'=2] {'sub','rep'}, dimensions={0} | all-to-all | bytes 589824 | tf_op jit(solution)/shard_map/all_to_all | solution.py:413
  15.2 0.0 copy-done
  15.3 0.0 copy-done.1
  15.3 2.1 %forecast.1 = (f32[1024,128]{1,0:T(8,128)S(1)}, f32[8,128]{1,0:T(8,128)S(1)}) custom-call(f32[512,256]{1,0:T(8,128)S(1)} %bitcast.13, f32[64,256]{1,0:T(8,128)S(1)} %copy-done.1, f32[576,128]{1,0:T(8,128)S(1)} %bitcast.17), custom_call_target="tpu_custom_call" | custom-call | flops 1000000 | bytes 1000000 | tf_op jit(solution)/shard_map/forecast/pallas_call | solution.py:414
  17.3 47.8 %all_to_all.16 = f32[64,16,128]{2,1,0:T(8,128)S(1)} all-to-all(f32[64,16,128]{2,1,0:T(8,128)S(1)} %bitcast.19), channel_id=1, replica_groups=mesh['grp_0'=16,'grp_1'=4,'sub'=4,'rep'=2] {'grp_0','grp_1'}, dimensions={0} | all-to-all | bytes 1048576 | tf_op jit(solution)/shard_map/all_to_all | solution.py:421
  65.1 3.9 %analysis.1 = f32[1024,128]{1,0:T(8,128)S(1)} custom-call(f32[1024,128]{1,0:T(8,128)S(1)} %bitcast.14, f32[8,128]{1,0:T(8,128)S(1)} %get-tuple-element.8.slots_ref), custom_call_target="tpu_custom_call" | custom-call | flops 1000000 | bytes 1000000 | tf_op jit(solution)/shard_map/analysis/pallas_call | solution.py:422
  69.0 37.7 %all_to_all.17 = f32[64,16,128]{2,1,0:T(8,128)S(1)} all-to-all(f32[64,16,128]{2,1,0:T(8,128)S(1)} %bitcast.15), channel_id=1, replica_groups=mesh['grp_0'=16,'grp_1'=4,'sub'=4,'rep'=2] {'grp_0','grp_1'}, dimensions={0} | all-to-all | bytes 1048576 | tf_op jit(solution)/shard_map/all_to_all | solution.py:429
  106.7 0.9 unpack.1
Async XLA Ops:
  0.0 15.2 %copy-start = (f32[1,8,64,256]{3,2,1,0:T(8,128)S(1)}, f32[1,8,64,256]{3,2,1,0:T(8,128)}, u32[]{:S(2)}) copy-start(f32[1,8,64,256]{3,2,1,0:T(8,128)} %param.7) | copy-start | bytes 1572868
  1.3 13.9 %copy-start.1 = (f32[64,256]{1,0:T(8,128)S(1)}, f32[64,256]{1,0:T(8,128)}, u32[]{:S(2)}) copy-start(f32[64,256]{1,0:T(8,128)} %d_ref.3) | copy-start | bytes 196612

commit v5 on v4

--- a/solution.py
+++ b/solution.py
@@ -20,6 +20,7 @@
 VMEM_LIMIT = 24 * 1024 * 1024
 SUBS = 4
 BLOCK = 72
+TURN = 44
 
 
 def pack_kernel(
@@ -164,7 +165,7 @@
                 d_row = w_ref[80 * t + row + STEPS : 80 * t + row + STEPS + 1, :]
                 new = centre[t] + d_row * spread - winds[t] * (centre[t] - west)
                 if final:
-                    at = 16 * (row - skip) + 8 * t
+                    at = 16 * ((row - skip - TURN) % ROWS) + 8 * t
                     out_ref[at : at + 8, :] = new
                 else:
                     at = 24 * row + 8 * t
@@ -342,7 +343,13 @@
     for l in range(LEVELS):
         rows = slice(ROWS * l, ROWS * (l + 1))
         for h in range(2):
-            out_ref[rows, h * PATCH : (h + 1) * PATCH] = x_ref[pl.ds(8 * h + l, ROWS, stride=16), :]
+            cols = slice(h * PATCH, (h + 1) * PATCH)
+            base = 8 * h + l
+            if TURN:
+                out_ref[rows.start : rows.start + TURN, cols] = x_ref[
+                    pl.ds(16 * (ROWS - TURN) + base, TURN, stride=16), :
+                ]
+            out_ref[rows.start + TURN : rows.stop, cols] = x_ref[pl.ds(base, ROWS - TURN, stride=16), :]
         if l % 2:
             some = pl.ds(ROWS * (l - 1), 2 * ROWS)
             copies.append(pltpu.make_async_copy(out_ref.at[some], out_hbm.at[some], sems.at[l // 2]))
@@ -371,6 +378,12 @@
         cost_estimate=pl.CostEstimate(flops=flops, bytes_accessed=1_000_000, transcendentals=0),
         name=name,
     )
+
+
+def exchange(x):
+    z, inner = lax.axis_size("grp_0") * lax.axis_size("grp_1"), lax.axis_size("sub") * lax.axis_size("rep")
+    groups = [[(g + TURN) % z * inner + i for g in range(z)] for i in range(inner)]
+    return lax.all_to_all(x, ("grp_0", "grp_1", "sub", "rep"), 0, 0, axis_index_groups=groups, tiled=True)
 
 
 def on_device(start, diffusivity, stability, observed, variance, site, live):
@@ -418,7 +431,7 @@
         scratch=[vmem(24 * TALL, PATCH), vmem(24 * TALL, PATCH), vmem(3 * (ROWS + 16), PATCH)],
         name="forecast",
     )(start.reshape(LEVELS * ROWS, COLS), diffusivity, got.reshape(2 * SUBS * BLOCK, PATCH))
-    gathered = lax.all_to_all(forecast.reshape(ROWS, 16, PATCH), GRP, 0, 0, tiled=True)
+    gathered = exchange(forecast.reshape(ROWS, 16, PATCH))
     analysed = call(
         analysis_kernel,
         [f32(MEMBERS * 16, PATCH)],
@@ -426,7 +439,7 @@
         scratch=[pltpu.VMEM((2 * MEMBERS, LEVELS * PATCH), jnp.float32)],
         name="analysis",
     )(gathered.reshape(MEMBERS * 16, PATCH), slots)
-    returned = lax.all_to_all(analysed.reshape(MEMBERS, 16, PATCH), GRP, 0, 0, tiled=True)
+    returned = exchange(analysed.reshape(MEMBERS, 16, PATCH))
     out = call(
         unpack_kernel,
         [f32(LEVELS * ROWS, COLS)],

time: 110 us -> 103 us (0.936)
  blocking collectives: 99.4 us -> 93.1 us
    all_to_all x2, blocking collectives: 85.5 us -> 79.2 us  [exchange(): lax.all_to_all(x, ('grp_0', 'grp_1', 'sub', 'rep'), 0, 0, axis_index_grou...]
where the time goes in v5:
time: 103 us; the launch traced here: 101 us
  blocking collectives  93.1 us (90%)
  Pallas kernels  8.09 us (8%)
    all_to_all x2, blocking collectives, exchange(): lax.all_to_all(x, ('grp_0', 'grp_1', 'sub', 'rep'), 0, 0, axis_index_grou...  79.2 us
    all_to_all x1, blocking collectives, on_device(): lax.all_to_all(send.reshape(2 * SUBS, BLOCK, PATCH), ('sub', 'rep'), 0, 0...  13.9 us
    pallas_call x1, Pallas kernels, on_device(): call(analysis_kernel, [f32(MEMBERS * 16, PATCH)], [VMEM] * 2, scratch=[pl...  3.85 us
    pallas_call x1, Pallas kernels, on_device(): call(forecast_kernel, [f32(ROWS * 16, PATCH), f32(8, PATCH)], [VMEM] * 3,...  2.06 us

profile of v5, /device:TPU:24, one launch (start us, length us, event | category | flops | bytes accessed | tf_op | source)
XLA Modules:
  0.0 101.2 jit_solution(2261130262871865925)
XLA Ops:
  0.0 0.0 copy-start
  0.0 1.3 %pack.1 = f32[576,128]{1,0:T(8,128)S(1)} custom-call(f32[8,64,256]{2,1,0:T(8,128)} %bitcast.12, f32[64,256]{1,0:T(8,128)} %d_ref.3, f32[1,8]{1,0:T(1,128)} %stability_ref.1, f32[2,128]{1,0:T(2,128)} %bitcast.20, f32[2,128]{1,0:T(2,128)} %bitcast.21, s32[2,128]{1,0:T(2,128)} %bitcast.22, s32[1,2]{1,0:T(1,128)} %count_hbm.1), custom_call_target="tpu_custom_call" | custom-call | flops 1000000 | bytes 1000000 | tf_op jit(solution)/shard_map/pack/pallas_call | solution.py:393
  1.3 0.0 copy-start.1
  1.3 13.9 %all_to_all.15 = f32[8,72,128]{2,1,0:T(8,128)S(1)} all-to-all(f32[8,72,128]{2,1,0:T(8,128)S(1)} %bitcast.18), channel_id=1, replica_groups=mesh['grp_0'=16,'grp_1'=4,'sub'=4,'rep'=2] {'sub','rep'}, dimensions={0} | all-to-all | bytes 589824 | tf_op jit(solution)/shard_map/all_to_all | solution.py:426
  15.2 0.0 copy-done
  15.3 0.0 copy-done.1
  15.3 2.1 %forecast.1 = (f32[1024,128]{1,0:T(8,128)S(1)}, f32[8,128]{1,0:T(8,128)S(1)}) custom-call(f32[512,256]{1,0:T(8,128)S(1)} %bitcast.13, f32[64,256]{1,0:T(8,128)S(1)} %copy-done.1, f32[576,128]{1,0:T(8,128)S(1)} %bitcast.17), custom_call_target="tpu_custom_call" | custom-call | flops 1000000 | bytes 1000000 | tf_op jit(solution)/shard_map/forecast/pallas_call | solution.py:427
  17.3 40.8 %all_to_all.16 = f32[64,16,128]{2,1,0:T(8,128)S(1)} all-to-all(f32[64,16,128]{2,1,0:T(8,128)S(1)} %bitcast.19), channel_id=1, replica_groups={{352,360,368,376,384,392,400,408,416,424,432,440,448,456,464,472,480,48..., dimensions={0} | all-to-all | bytes 1048576 | tf_op jit(solution)/shard_map/all_to_all | solution.py:386
  58.1 3.9 %analysis.1 = f32[1024,128]{1,0:T(8,128)S(1)} custom-call(f32[1024,128]{1,0:T(8,128)S(1)} %bitcast.14, f32[8,128]{1,0:T(8,128)S(1)} %get-tuple-element.8.slots_ref), custom_call_target="tpu_custom_call" | custom-call | flops 1000000 | bytes 1000000 | tf_op jit(solution)/shard_map/analysis/pallas_call | solution.py:435
  62.0 38.4 %all_to_all.17 = f32[64,16,128]{2,1,0:T(8,128)S(1)} all-to-all(f32[64,16,128]{2,1,0:T(8,128)S(1)} %bitcast.15), channel_id=1, replica_groups={{352,360,368,376,384,392,400,408,416,424,432,440,448,456,464,472,480,48..., dimensions={0} | all-to-all | bytes 1048576 | tf_op jit(solution)/shard_map/all_to_all | solution.py:386
  100.4 0.9 unpack.1
Async XLA Ops:
  0.0 15.2 %copy-start = (f32[1,8,64,256]{3,2,1,0:T(8,128)S(1)}, f32[1,8,64,256]{3,2,1,0:T(8,128)}, u32[]{:S(2)}) copy-start(f32[1,8,64,256]{3,2,1,0:T(8,128)} %param.7) | copy-start | bytes 1572868
  1.3 13.9 %copy-start.1 = (f32[64,256]{1,0:T(8,128)S(1)}, f32[64,256]{1,0:T(8,128)}, u32[]{:S(2)}) copy-start(f32[64,256]{1,0:T(8,128)} %d_ref.3) | copy-start | bytes 196612

commit v6 on v5

--- a/solution.py
+++ b/solution.py
@@ -20,7 +20,11 @@
 VMEM_LIMIT = 24 * 1024 * 1024
 SUBS = 4
 BLOCK = 72
-TURN = 44
+TURN = 46
+
+
+def block(y, rep):
+    return pl.multiple_of(BLOCK * (2 * y + 1 - rep), 8)
 
 
 def pack_kernel(
@@ -53,9 +57,8 @@
     lane = lax.broadcasted_iota(jnp.int32, (8, PATCH), 1)
     for copy in copies:
         copy.wait()
-    me = 2 * y + rep
-    away = 2 * lax.rem(y + 2, SUBS) + rep
-    side_at = pl.multiple_of(BLOCK * (2 * y + 1 - rep), 8)
+    away = lax.rem(y + 2, SUBS)
+    side_at = block(y, 1 - rep)
     for l in range(LEVELS + 1):
         packed = jnp.zeros((8, PATCH), jnp.float32)
         for r in range(8):
@@ -68,8 +71,8 @@
         (y > 0, -1, top_ref, dtop_ref, 0),
         (y < SUBS - 1, 1, end_ref, dend_ref, 8 - STEPS),
     ):
-        at = pl.multiple_of(BLOCK * jnp.where(ok, me + 2 * step, away), 8)
-        corner = pl.multiple_of(BLOCK * jnp.where(ok, 2 * (y + step) + 1 - rep, away), 8)
+        there_y = jnp.where(ok, y + step, away)
+        at, corner = block(there_y, rep), block(there_y, 1 - rep)
         for l in range(LEVELS):
             send_ref[pl.ds(corner + l, STEPS, stride=8), :] = edge_ref[
                 l, (first // 4) * (ROWS - 8) + first : (first // 4) * (ROWS - 8) + first + STEPS, :
@@ -84,7 +87,7 @@
                     l, first : first + STEPS, cols
                 ]
             send_ref[pl.ds(at + 64 + STEPS * h, STEPS), :] = d_rows[first : first + STEPS, cols]
-    own = pl.multiple_of(BLOCK * me, 8)
+    own = block(y, rep)
     picked = jnp.where(sub_id[:, :8] == lane[:, :8], calm_ref[...], 0.0)
     send_ref[pl.ds(own, 8), :] = jnp.broadcast_to(jnp.sum(picked, axis=1, keepdims=True), (LEVELS, PATCH))
     send_ref[pl.ds(own + 8, 2), :] = obs_ref[...]
@@ -99,9 +102,8 @@
     lane = lax.broadcasted_iota(jnp.int32, (8, PATCH), 1)
     low = jnp.where(rep == 0, 0, PATCH - STEPS)
     keep = (lane >= low) & (lane < low + STEPS)
-    me = 2 * y + rep
-    away = 2 * lax.rem(y + 2, SUBS) + rep
-    side_at = pl.multiple_of(BLOCK * (2 * y + 1 - rep), 8)
+    away = lax.rem(y + 2, SUBS)
+    side_at = block(y, 1 - rep)
     own = 24 * STEPS
     for l in range(LEVELS + 1):
         packed = got_ref[pl.ds(side_at + 8 * l, 8), :]
@@ -123,8 +125,8 @@
         (y > 0, -1, 0, STEPS),
         (y < SUBS - 1, 1, STEPS + ROWS, 8 + ROWS),
     ):
-        at = pl.multiple_of(BLOCK * jnp.where(ok, me + 2 * step, away), 8)
-        corner = pl.multiple_of(BLOCK * jnp.where(ok, 2 * (y + step) + 1 - rep, away), 8)
+        there_y = jnp.where(ok, y + step, away)
+        at, corner = block(there_y, rep), block(there_y, 1 - rep)
         there = jnp.broadcast_to(ok, (8, PATCH))
         both = keep & there
         for r in range(STEPS):
@@ -139,7 +141,7 @@
             w_ref[80 * t + d_base : 80 * t + d_base + STEPS, :] = rows[STEPS * t : STEPS * (t + 1)]
         rows = jnp.where(both, got_ref[pl.ds(corner + 32, 8), :], 0.0)
         w_ref[160 + d_base : 160 + d_base + STEPS, :] = rows[:STEPS]
-    mine = pl.multiple_of(BLOCK * me, 8)
+    mine = block(y, rep)
     wind = got_ref[pl.ds(mine, 8), :]
     slots_ref[...] = got_ref[pl.ds(mine + 8, 8), :]
     winds = [wind, wind, jnp.where(keep, wind, 0.0)]
@@ -383,6 +385,12 @@
 def exchange(x):
     z, inner = lax.axis_size("grp_0") * lax.axis_size("grp_1"), lax.axis_size("sub") * lax.axis_size("rep")
     groups = [[(g + TURN) % z * inner + i for g in range(z)] for i in range(inner)]
+    return lax.all_to_all(x, ("grp_0", "grp_1", "sub", "rep"), 0, 0, axis_index_groups=groups, tiled=True)
+
+
+def swap_ends(x):
+    grp = lax.axis_size("grp_0") * lax.axis_size("grp_1")
+    groups = [[2 * (SUBS * g + y) + rep for y in range(SUBS) for rep in (1, 0)] for g in range(grp)]
     return lax.all_to_all(x, ("grp_0", "grp_1", "sub", "rep"), 0, 0, axis_index_groups=groups, tiled=True)
 
 
@@ -423,7 +431,7 @@
             )
         )
     )
-    got = lax.all_to_all(send.reshape(2 * SUBS, BLOCK, PATCH), ("sub", "rep"), 0, 0, tiled=True)
+    got = swap_ends(send.reshape(2 * SUBS, BLOCK, PATCH))
     forecast, slots = call(
         forecast_kernel,
         [f32(ROWS * 16, PATCH), f32(8, PATCH)],

time: 103 us -> 102 us (level)
    all_to_all x1, blocking collectives: 13.9 us -> 12.7 us  [swap_ends(): lax.all_to_all(x, ('grp_0', 'grp_1', 'sub', 'rep'), 0, 0, axis_index_grou...]
where the time goes in v6:
time: 102 us; the launch traced here: 101 us
  blocking collectives  92.5 us (91%)
  Pallas kernels  8.09 us (8%)
    all_to_all x2, blocking collectives, exchange(): lax.all_to_all(x, ('grp_0', 'grp_1', 'sub', 'rep'), 0, 0, axis_index_grou...  79.8 us
    all_to_all x1, blocking collectives, swap_ends(): lax.all_to_all(x, ('grp_0', 'grp_1', 'sub', 'rep'), 0, 0, axis_index_grou...  12.7 us
    pallas_call x1, Pallas kernels, on_device(): call(analysis_kernel, [f32(MEMBERS * 16, PATCH)], [VMEM] * 2, scratch=[pl...  3.85 us
    pallas_call x1, Pallas kernels, on_device(): call(forecast_kernel, [f32(ROWS * 16, PATCH), f32(8, PATCH)], [VMEM] * 3,...  2.07 us

profile of v6, /device:TPU:24, one launch (start us, length us, event | category | flops | bytes accessed | tf_op | source)
XLA Modules:
  0.0 100.6 jit_solution(13054553880617984841)
XLA Ops:
  0.0 0.0 copy-start
  0.0 1.3 %pack.1 = f32[576,128]{1,0:T(8,128)S(1)} custom-call(f32[8,64,256]{2,1,0:T(8,128)} %bitcast.12, f32[64,256]{1,0:T(8,128)} %d_ref.3, f32[1,8]{1,0:T(1,128)} %stability_ref.1, f32[2,128]{1,0:T(2,128)} %bitcast.20, f32[2,128]{1,0:T(2,128)} %bitcast.21, s32[2,128]{1,0:T(2,128)} %bitcast.22, s32[1,2]{1,0:T(1,128)} %count_hbm.1), custom_call_target="tpu_custom_call" | custom-call | flops 1000000 | bytes 1000000 | tf_op jit(solution)/shard_map/pack/pallas_call | solution.py:401
  1.3 0.0 copy-start.1
  1.3 12.7 %all_to_all.15 = f32[8,72,128]{2,1,0:T(8,128)S(1)} all-to-all(f32[8,72,128]{2,1,0:T(8,128)S(1)} %bitcast.18), channel_id=1, replica_groups={{1,0,3,2,5,4,7,6},{9,8,11,10,13,12,15,14},{17,16,19,18,21,20,23,22},{25..., dimensions={0} | all-to-all | bytes 589824 | tf_op jit(solution)/shard_map/all_to_all | solution.py:394
  14.0 0.0 copy-done
  14.0 0.0 copy-done.1
  14.0 2.1 %forecast.1 = (f32[1024,128]{1,0:T(8,128)S(1)}, f32[8,128]{1,0:T(8,128)S(1)}) custom-call(f32[512,256]{1,0:T(8,128)S(1)} %bitcast.13, f32[64,256]{1,0:T(8,128)S(1)} %copy-done.1, f32[576,128]{1,0:T(8,128)S(1)} %bitcast.17), custom_call_target="tpu_custom_call" | custom-call | flops 1000000 | bytes 1000000 | tf_op jit(solution)/shard_map/forecast/pallas_call | solution.py:435
  16.1 42.0 %all_to_all.16 = f32[64,16,128]{2,1,0:T(8,128)S(1)} all-to-all(f32[64,16,128]{2,1,0:T(8,128)S(1)} %bitcast.19), channel_id=1, replica_groups={{368,376,384,392,400,408,416,424,432,440,448,456,464,472,480,488,496,50..., dimensions={0} | all-to-all | bytes 1048576 | tf_op jit(solution)/shard_map/all_to_all | solution.py:388
  58.1 3.8 %analysis.1 = f32[1024,128]{1,0:T(8,128)S(1)} custom-call(f32[1024,128]{1,0:T(8,128)S(1)} %bitcast.14, f32[8,128]{1,0:T(8,128)S(1)} %get-tuple-element.8.slots_ref), custom_call_target="tpu_custom_call" | custom-call | flops 1000000 | bytes 1000000 | tf_op jit(solution)/shard_map/analysis/pallas_call | solution.py:443
  62.0 37.8 %all_to_all.17 = f32[64,16,128]{2,1,0:T(8,128)S(1)} all-to-all(f32[64,16,128]{2,1,0:T(8,128)S(1)} %bitcast.15), channel_id=1, replica_groups={{368,376,384,392,400,408,416,424,432,440,448,456,464,472,480,488,496,50..., dimensions={0} | all-to-all | bytes 1048576 | tf_op jit(solution)/shard_map/all_to_all | solution.py:388
  99.7 0.9 unpack.1
Async XLA Ops:
  0.0 14.0 %copy-start = (f32[1,8,64,256]{3,2,1,0:T(8,128)S(1)}, f32[1,8,64,256]{3,2,1,0:T(8,128)}, u32[]{:S(2)}) copy-start(f32[1,8,64,256]{3,2,1,0:T(8,128)} %param.7) | copy-start | bytes 1572868
  1.3 12.7 %copy-start.1 = (f32[64,256]{1,0:T(8,128)S(1)}, f32[64,256]{1,0:T(8,128)}, u32[]{:S(2)}) copy-start(f32[64,256]{1,0:T(8,128)} %d_ref.3) | copy-start | bytes 196612

commit v7 on v6

--- a/solution.py
+++ b/solution.py
@@ -55,7 +55,7 @@
         copy.start()
     sub_id = lax.broadcasted_iota(jnp.int32, (8, PATCH), 0)
     lane = lax.broadcasted_iota(jnp.int32, (8, PATCH), 1)
-    for copy in copies:
+    for copy in copies[:2]:
         copy.wait()
     away = lax.rem(y + 2, SUBS)
     side_at = block(y, 1 - rep)
@@ -67,6 +67,8 @@
             turned = pltpu.roll(tile, lax.rem(16 * (r + 1 - rep), PATCH), 1)
             packed = jnp.where(lane // 16 == r, turned, packed)
         send_ref[pl.ds(side_at + 8 * l, 8), :] = packed
+    for copy in copies[2:6]:
+        copy.wait()
     for ok, step, rows_ref, d_rows, first in (
         (y > 0, -1, top_ref, dtop_ref, 0),
         (y < SUBS - 1, 1, end_ref, dend_ref, 8 - STEPS),
@@ -87,6 +89,8 @@
                     l, first : first + STEPS, cols
                 ]
             send_ref[pl.ds(at + 64 + STEPS * h, STEPS), :] = d_rows[first : first + STEPS, cols]
+    for copy in copies[6:]:
+        copy.wait()
     own = block(y, rep)
     picked = jnp.where(sub_id[:, :8] == lane[:, :8], calm_ref[...], 0.0)
     send_ref[pl.ds(own, 8), :] = jnp.broadcast_to(jnp.sum(picked, axis=1, keepdims=True), (LEVELS, PATCH))

time: 102 us -> 102 us (level)
  no operation moved by 1% of the time
where the time goes in v7:
time: 102 us; the launch traced here: 101 us
  blocking collectives  92.5 us (91%)
  Pallas kernels  8.2 us (8%)
    all_to_all x2, blocking collectives, exchange(): lax.all_to_all(x, ('grp_0', 'grp_1', 'sub', 'rep'), 0, 0, axis_index_grou...  79.8 us
    all_to_all x1, blocking collectives, swap_ends(): lax.all_to_all(x, ('grp_0', 'grp_1', 'sub', 'rep'), 0, 0, axis_index_grou...  12.7 us
    pallas_call x1, Pallas kernels, on_device(): call(analysis_kernel, [f32(MEMBERS * 16, PATCH)], [VMEM] * 2, scratch=[pl...  3.86 us
    pallas_call x1, Pallas kernels, on_device(): call(forecast_kernel, [f32(ROWS * 16, PATCH), f32(8, PATCH)], [VMEM] * 3,...  2.07 us

profile of v7, /device:TPU:24, one launch (start us, length us, event | category | flops | bytes accessed | tf_op | source)
XLA Modules:
  0.0 100.7 jit_solution(16617786736865096982)
XLA Ops:
  0.0 0.0 copy-start
  0.0 1.4 %pack.1 = f32[576,128]{1,0:T(8,128)S(1)} custom-call(f32[8,64,256]{2,1,0:T(8,128)} %bitcast.12, f32[64,256]{1,0:T(8,128)} %d_ref.3, f32[1,8]{1,0:T(1,128)} %stability_ref.1, f32[2,128]{1,0:T(2,128)} %bitcast.20, f32[2,128]{1,0:T(2,128)} %bitcast.21, s32[2,128]{1,0:T(2,128)} %bitcast.22, s32[1,2]{1,0:T(1,128)} %count_hbm.1), custom_call_target="tpu_custom_call" | custom-call | flops 1000000 | bytes 1000000 | tf_op jit(solution)/shard_map/pack/pallas_call | solution.py:405
  1.4 0.0 copy-start.1
  1.4 12.7 %all_to_all.15 = f32[8,72,128]{2,1,0:T(8,128)S(1)} all-to-all(f32[8,72,128]{2,1,0:T(8,128)S(1)} %bitcast.18), channel_id=1, replica_groups={{1,0,3,2,5,4,7,6},{9,8,11,10,13,12,15,14},{17,16,19,18,21,20,23,22},{25..., dimensions={0} | all-to-all | bytes 589824 | tf_op jit(solution)/shard_map/all_to_all | solution.py:398
  14.1 0.0 copy-done
  14.1 0.0 copy-done.1
  14.1 2.1 %forecast.1 = (f32[1024,128]{1,0:T(8,128)S(1)}, f32[8,128]{1,0:T(8,128)S(1)}) custom-call(f32[512,256]{1,0:T(8,128)S(1)} %bitcast.13, f32[64,256]{1,0:T(8,128)S(1)} %copy-done.1, f32[576,128]{1,0:T(8,128)S(1)} %bitcast.17), custom_call_target="tpu_custom_call" | custom-call | flops 1000000 | bytes 1000000 | tf_op jit(solution)/shard_map/forecast/pallas_call | solution.py:439
  16.2 42.0 %all_to_all.16 = f32[64,16,128]{2,1,0:T(8,128)S(1)} all-to-all(f32[64,16,128]{2,1,0:T(8,128)S(1)} %bitcast.19), channel_id=1, replica_groups={{368,376,384,392,400,408,416,424,432,440,448,456,464,472,480,488,496,50..., dimensions={0} | all-to-all | bytes 1048576 | tf_op jit(solution)/shard_map/all_to_all | solution.py:392
  58.2 3.9 %analysis.1 = f32[1024,128]{1,0:T(8,128)S(1)} custom-call(f32[1024,128]{1,0:T(8,128)S(1)} %bitcast.14, f32[8,128]{1,0:T(8,128)S(1)} %get-tuple-element.8.slots_ref), custom_call_target="tpu_custom_call" | custom-call | flops 1000000 | bytes 1000000 | tf_op jit(solution)/shard_map/analysis/pallas_call | solution.py:447
  62.1 37.8 %all_to_all.17 = f32[64,16,128]{2,1,0:T(8,128)S(1)} all-to-all(f32[64,16,128]{2,1,0:T(8,128)S(1)} %bitcast.15), channel_id=1, replica_groups={{368,376,384,392,400,408,416,424,432,440,448,456,464,472,480,488,496,50..., dimensions={0} | all-to-all | bytes 1048576 | tf_op jit(solution)/shard_map/all_to_all | solution.py:392
  99.8 0.9 unpack.1
Async XLA Ops:
  0.0 14.1 %copy-start = (f32[1,8,64,256]{3,2,1,0:T(8,128)S(1)}, f32[1,8,64,256]{3,2,1,0:T(8,128)}, u32[]{:S(2)}) copy-start(f32[1,8,64,256]{3,2,1,0:T(8,128)} %param.7) | copy-start | bytes 1572868
  1.4 12.7 %copy-start.1 = (f32[64,256]{1,0:T(8,128)S(1)}, f32[64,256]{1,0:T(8,128)}, u32[]{:S(2)}) copy-start(f32[64,256]{1,0:T(8,128)} %d_ref.3) | copy-start | bytes 196612
